TPU v7x, 32 devices: a whole 2x2x4 slice. The times are simulated.
32 devices in a mesh: groups: 2 (over y), row: 16 (over z, x, core).
Axes of the slice: x: 2, y: 2, z: 4, core: 2. Of those that a mesh axis runs over, the one named last changes fastest.
Arguments:
- attn_out: bfloat16 [256, 8192], P('groups', 'row'), parts along dimension 0, may hold values from -6 to 6
- residual_in: bfloat16 [16, 128, 1024], P('row', 'groups'), parts along dimension 1, may hold values from -32 to 32
- out_weight: bfloat16 [16, 4096, 1024], P('row'), may hold values from -0.0625 to 0.0625
- norm_gain: float32 [8192], replicated, may hold values from 0.1 to 1.9
- gate_weight: bfloat16 [16, 1024, 7168], P('row'), may hold values from -0.0625 to 0.0625
- up_weight: bfloat16 [16, 1024, 7168], P('row'), may hold values from -0.0625 to 0.0625
- down_weight: bfloat16 [16, 7168, 1024], P('row'), may hold values from -0.046875 to 0.046875
Outputs:
- layer_out: bfloat16 [256, 16, 512], P('groups', 'row'), parts along dimension 0
There are 2 independent parts, one for each index of `groups`. A program takes and returns all parts, laid end to end along the dimension named above; an argument that names none is the same for every part. Nothing has to cross between parts.
All inputs are finite; a program needn't handle non-finite values.
Results may differ from a plain program's by a relative error of at most 0.0055.
Values may be sent and summed in bfloat16 or wider, within the bound.
A program may use at most 128 MiB of HBM per device.

v0:
```python
import jax
import jax.numpy as jnp
from jax import lax
from jax.sharding import PartitionSpec as P

D = 8192
COLG = 8


def from_partner(value, axis, stride):
    mask = 2**stride
    pairs = [(source, source ^ mask) for source in range(lax.axis_size(axis))]
    return lax.ppermute(value, axis, pairs)


def gather_bits(value, dim, bit_list, device_pos, sender):
    for bit_pos in bit_list:
        incoming = sender(value, bit_pos)
        on_low = device_pos >> bit_pos & 1 == 0
        value = jnp.where(
            on_low, jnp.concatenate([value, incoming], dim), jnp.concatenate([incoming, value], dim)
        )
    return value


def reduce_bits(value, dim, bit_list, device_pos, sender):
    for bit_pos in reversed(bit_list):
        middle = value.shape[dim] // 2
        bottom = lax.slice_in_dim(value, 0, middle, axis=dim)
        top_part = lax.slice_in_dim(value, middle, 2 * middle, axis=dim)
        on_low = device_pos >> bit_pos & 1 == 0
        kept = jnp.where(on_low, bottom, top_part)
        outgoing = jnp.where(on_low, top_part, bottom)
        value = kept + sender(outgoing, bit_pos)
    return value


def sum_bits(value, bit_list, sender):
    for bit_pos in bit_list:
        value = value + sender(value, bit_pos)
    return value


def local(attn_out, residual_in, out_weight, norm_gain, gate_weight, up_weight, down_weight):
    all_bits = lax.axis_size("row").bit_length() - 1
    col_count = COLG.bit_length() - 1
    col_bits = list(range(col_count))
    row_bits = list(range(col_count, all_bits))
    device_pos = lax.axis_index("row")
    col_index = device_pos % COLG
    row_index = device_pos // COLG
    panel_in = gather_bits(
        attn_out,
        1,
        col_bits,
        device_pos,
        lambda block_piece, bit_pos: from_partner(block_piece, "row", bit_pos),
    )
    partial_proj = jnp.dot(panel_in, out_weight[0], preferred_element_type=jnp.float32)
    projected = reduce_bits(
        partial_proj,
        0,
        row_bits,
        device_pos,
        lambda block_piece, bit_pos: from_partner(block_piece, "row", bit_pos),
    )
    stream = (residual_in[0].astype(jnp.float32) + projected).astype(jnp.bfloat16)
    widened = stream.astype(jnp.float32)
    feat_cols = widened.shape[1]
    squares = jnp.sum(widened * widened, axis=-1)
    squares = sum_bits(
        squares, col_bits, lambda block_piece, bit_pos: from_partner(block_piece, "row", bit_pos)
    )
    mean_square = (squares / D)[:, None]
    gain_part = lax.dynamic_slice_in_dim(norm_gain, col_index * feat_cols, feat_cols)
    normed = (widened * lax.rsqrt(mean_square + 1e-05) * gain_part).astype(jnp.bfloat16)
    token_rows = gather_bits(
        normed,
        0,
        row_bits,
        device_pos,
        lambda block_piece, bit_pos: from_partner(block_piece, "row", bit_pos),
    )
    gate_vals = jnp.dot(token_rows, gate_weight[0], preferred_element_type=jnp.float32)
    up_vals = jnp.dot(token_rows, up_weight[0], preferred_element_type=jnp.float32)
    stacked = jnp.stack([gate_vals, up_vals])
    summed = reduce_bits(
        stacked,
        1,
        col_bits,
        device_pos,
        lambda block_piece, bit_pos: from_partner(block_piece, "row", bit_pos),
    )
    hidden = (jax.nn.silu(summed[0]) * summed[1]).astype(jnp.bfloat16)
    hidden_rows = gather_bits(
        hidden,
        0,
        col_bits,
        device_pos,
        lambda block_piece, bit_pos: from_partner(block_piece, "row", bit_pos),
    )
    partial_down = jnp.dot(hidden_rows, down_weight[0], preferred_element_type=jnp.float32)
    piece_width = feat_cols // 2 ** len(row_bits)
    stream_rows = gather_bits(
        stream,
        0,
        row_bits,
        device_pos,
        lambda block_piece, bit_pos: from_partner(block_piece, "row", bit_pos),
    )
    stream_piece = lax.dynamic_slice_in_dim(stream_rows, row_index * piece_width, piece_width, 1)
    down_piece = reduce_bits(
        partial_down,
        1,
        row_bits,
        device_pos,
        lambda block_piece, bit_pos: from_partner(block_piece, "row", bit_pos),
    )
    result = (stream_piece.astype(jnp.float32) + down_piece).astype(jnp.bfloat16)
    return result[:, None, :]


def solution(mesh):
    in_specs = (
        P("groups", "row"),
        P("row", "groups", None),
        P("row", None, None),
        P(),
        P("row", None, None),
        P("row", None, None),
        P("row", None, None),
    )
    out_specs = P("groups", "row", None)
    return jax.shard_map(local, mesh=mesh, in_specs=in_specs, out_specs=out_specs, check_vma=False)
```

profile of v0, /device:TPU:0, one launch (start us, length us, event | category | flops | bytes accessed | tf_op | source)
XLA Modules:
  0.0 253.0 jit_solution(12165477187889464021)
XLA Ops:
  0.0 0.5 collective-permute-start
  0.5 1.2 collective-permute-done
  1.7 1.0 maximum_select_fusion.7
  2.7 2.9 %collective-permute-start.1 = (bf16[128,1024]{1,0:T(8,128)(2,1)S(1)}, bf16[128,1024]{1,0:T(8,128)(2,1)S(1)}, u32[]{:S(2)}, u32[]{:S(2)}) collective-permute-start(bf16[128,1024]{1,0:T(8,128)(2,1)S(1)} %maximum_select_fusion.7), channel_id=1, source_target_pairs={{0,2},{1,3},{2,0},{3,1},{4,6},{5,7},{6,4},{7,5},{8,10},{9,11},{10,... | collective-permute-start | bytes 786440 | tf_op jit(solution)/shard_map/ppermute | solution.py:13
  5.6 6.6 %collective-permute-done.1 = bf16[128,1024]{1,0:T(8,128)(2,1)S(1)} collective-permute-done((bf16[128,1024]{1,0:T(8,128)(2,1)S(1)}, bf16[128,1024]{1,0:T(8,128)(2,1)S(1)}, u32[]{:S(2)}, u32[]{:S(2)}) %collective-permute-start.1) | collective-permute-done | bytes 262176 | tf_op jit(solution)/shard_map/ppermute | solution.py:13
  12.2 0.1 maximum_select_fusion.5
  12.4 1.9 collective-permute-start.2
  14.3 11.6 %collective-permute-done.2 = bf16[128,2048]{1,0:T(8,128)(2,1)S(1)} collective-permute-done((bf16[128,2048]{1,0:T(8,128)(2,1)S(1)}, bf16[128,2048]{1,0:T(8,128)(2,1)S(1)}, u32[]{:S(2)}, u32[]{:S(2)}) %collective-permute-start.2) | collective-permute-done | bytes 524320 | tf_op jit(solution)/shard_map/ppermute | solution.py:13
  25.9 4.6 %fusion.12 = f32[128,1024]{1,0:T(8,128)S(1)} fusion(bf16[1,4096,1024]{2,1,0:T(8,128)(2,1)} %param.9, bf16[128,2048]{1,0:T(8,128)(2,1)S(1)} %collective-permute-done.2, bf16[128,2048]{1,0:T(8,128)(2,1)S(1)} %maximum_select_fusion.5, pred[]{:T(512)S(6)} %eq.11), kind=kOutput, calls=%fused_computation.8 | convolution fusion | flops 1078460416 | bytes 9961473 | tf_op jit(solution)/shard_map/dot_general | solution.py:59
  30.6 2.6 %collective-permute-start.3 = (f32[64,1024]{1,0:T(8,128)S(1)}, f32[64,1024]{1,0:T(8,128)S(1)}, u32[]{:S(2)}, u32[]{:S(2)}) collective-permute-start(f32[64,1024]{1,0:T(8,128)S(1)} %slice_select_fusion.3), channel_id=1, source_target_pairs={{0,8},{1,9},{2,10},{3,11},{4,12},{5,13},{6,14},{7,15},{8,0},{9,1},... | collective-permute-start | bytes 786440 | tf_op jit(solution)/shard_map/ppermute | solution.py:13
  33.2 10.9 %collective-permute-done.3 = f32[64,1024]{1,0:T(8,128)S(1)} collective-permute-done((f32[64,1024]{1,0:T(8,128)S(1)}, f32[64,1024]{1,0:T(8,128)S(1)}, u32[]{:S(2)}, u32[]{:S(2)}) %collective-permute-start.3) | collective-permute-done | bytes 262176 | tf_op jit(solution)/shard_map/ppermute | solution.py:13
  44.1 0.2 fusion.29
  44.4 1.1 collective-permute-done.5
  45.5 1.1 collective-permute-start.6
  46.6 2.5 collective-permute-done.6
  49.0 0.3 collective-permute-start.7
  49.3 0.7 dynamic_slice.7
  50.0 2.6 %collective-permute-done.7 = f32[64]{0:T(128)S(1)} collective-permute-done((f32[64]{0:T(128)S(1)}, f32[64]{0:T(128)S(1)}, u32[]{:S(2)}, u32[]{:S(2)}) %collective-permute-start.7) | collective-permute-done | bytes 288 | tf_op jit(solution)/shard_map/ppermute | solution.py:13
  52.6 0.1 fusion.31
  52.7 1.7 collective-permute-start.8
  54.4 5.7 %collective-permute-done.8 = bf16[64,1024]{1,0:T(8,128)(2,1)S(1)} collective-permute-done((bf16[64,1024]{1,0:T(8,128)(2,1)S(1)}, bf16[64,1024]{1,0:T(8,128)(2,1)S(1)}, u32[]{:S(2)}, u32[]{:S(2)}) %collective-permute-start.8) | collective-permute-done | bytes 131104 | tf_op jit(solution)/shard_map/ppermute | solution.py:13
  60.0 7.3 %fusion.6 = f32[1,128,7168]{2,1,0:T(8,128)S(1)} fusion(bf16[1,1024,7168]{2,1,0:T(8,128)(2,1)} %param.11, bf16[64,1024]{1,0:T(8,128)(2,1)S(1)} %collective-permute-done.8, bf16[64,1024]{1,0:T(8,128)(2,1)S(1)} %fusion.31, pred[]{:T(512)S(6)} %eq.10), kind=kOutput, calls=%fused_computation.6 | convolution fusion | flops 1880227840 | bytes 18612224 | tf_op jit(solution)/shard_map/dot_general | solution.py:84
  67.3 7.3 %fusion.9 = f32[1,128,7168]{2,1,0:T(8,128)S(1)} fusion(bf16[1,1024,7168]{2,1,0:T(8,128)(2,1)} %param.12, bf16[64,1024]{1,0:T(8,128)(2,1)S(1)} %collective-permute-done.8, bf16[64,1024]{1,0:T(8,128)(2,1)S(1)} %fusion.31, pred[]{:T(512)S(6)} %eq.10), kind=kOutput, calls=%fused_computation.7 | convolution fusion | flops 1880227840 | bytes 18612224 | tf_op jit(solution)/shard_map/dot_general | solution.py:85
  74.5 0.6 broadcast_select_fusion
  75.2 78.0 %collective-permute-done.9 = f32[2,64,7168]{2,1,0:T(8,128)S(1)} collective-permute-done((f32[2,64,7168]{2,1,0:T(8,128)S(1)}, f32[2,64,7168]{2,1,0:T(8,128)S(1)}, u32[]{:S(2)}, u32[]{:S(2)}) %collective-permute-start.9) | collective-permute-done | bytes 3670048 | tf_op jit(solution)/shard_map/ppermute | solution.py:13
  153.2 0.7 select_add_fusion
  153.9 0.2 slice_select_fusion
  154.1 1.1 collective-permute-start.10
  155.3 36.7 %collective-permute-done.10 = f32[2,32,7168]{2,1,0:T(8,128)S(1)} collective-permute-done((f32[2,32,7168]{2,1,0:T(8,128)S(1)}, f32[2,32,7168]{2,1,0:T(8,128)S(1)}, u32[]{:S(2)}, u32[]{:S(2)}) %collective-permute-start.10) | collective-permute-done | bytes 1835040 | tf_op jit(solution)/shard_map/ppermute | solution.py:13
  191.9 0.3 select_add_fusion.1
  192.2 0.1 slice_select_fusion.1
  192.3 0.1 collective-permute-start.11
  192.4 2.5 collective-permute-done.11
  194.9 0.2 select_add_fusion.2
  195.1 0.1 fusion.28
  195.2 0.2 collective-permute-start.12
  195.4 1.4 collective-permute-done.12
  196.8 0.1 maximum_select_fusion.6
  196.8 1.1 collective-permute-start.13
  198.0 11.5 %collective-permute-done.13 = bf16[32,7168]{1,0:T(8,128)(2,1)S(1)} collective-permute-done((bf16[32,7168]{1,0:T(8,128)(2,1)S(1)}, bf16[32,7168]{1,0:T(8,128)(2,1)S(1)}, u32[]{:S(2)}, u32[]{:S(2)}) %collective-permute-start.13) | collective-permute-done | bytes 458784 | tf_op jit(solution)/shard_map/ppermute | solution.py:13
  209.5 0.2 maximum_select_fusion.4
  209.6 0.6 collective-permute-start.14
  210.2 21.0 %collective-permute-done.14 = bf16[64,7168]{1,0:T(8,128)(2,1)S(1)} collective-permute-done((bf16[64,7168]{1,0:T(8,128)(2,1)S(1)}, bf16[64,7168]{1,0:T(8,128)(2,1)S(1)}, u32[]{:S(2)}, u32[]{:S(2)}) %collective-permute-start.14) | collective-permute-done | bytes 917536 | tf_op jit(solution)/shard_map/ppermute | solution.py:13
  231.3 2.2 fusion
  233.5 2.2 collective-permute-start.15
  235.7 0.8 collective-permute-start.4
  236.5 15.8 %collective-permute-done.4 = bf16[64,1024]{1,0:T(8,128)(2,1)S(1)} collective-permute-done((bf16[64,1024]{1,0:T(8,128)(2,1)S(1)}, bf16[64,1024]{1,0:T(8,128)(2,1)S(1)}, u32[]{:S(2)}, u32[]{:S(2)}) %collective-permute-start.4) | collective-permute-done | bytes 131104 | tf_op jit(solution)/shard_map/ppermute | solution.py:13
  252.3 0.7 fusion.33
  (19 shorter events, 0.2 us)
Async XLA Ops:
  0.0 1.6 collective-permute-start
  2.7 9.5 %collective-permute-start.1 = (bf16[128,1024]{1,0:T(8,128)(2,1)S(1)}, bf16[128,1024]{1,0:T(8,128)(2,1)S(1)}, u32[]{:S(2)}, u32[]{:S(2)}) collective-permute-start(bf16[128,1024]{1,0:T(8,128)(2,1)S(1)} %maximum_select_fusion.7), channel_id=1, source_target_pairs={{0,2},{1,3},{2,0},{3,1},{4,6},{5,7},{6,4},{7,5},{8,10},{9,11},{10,... | collective-permute-start | bytes 786440 | tf_op jit(solution)/shard_map/ppermute | solution.py:13
  12.4 13.5 %collective-permute-start.2 = (bf16[128,2048]{1,0:T(8,128)(2,1)S(1)}, bf16[128,2048]{1,0:T(8,128)(2,1)S(1)}, u32[]{:S(2)}, u32[]{:S(2)}) collective-permute-start(bf16[128,2048]{1,0:T(8,128)(2,1)S(1)} %maximum_select_fusion.5), channel_id=1, source_target_pairs={{0,4},{1,5},{2,6},{3,7},{4,0},{5,1},{6,2},{7,3},{8,12},{9,13},{10,... | collective-permute-start | bytes 1572872 | tf_op jit(solution)/shard_map/ppermute | solution.py:13
  14.3 29.9 %copy-start = (bf16[1,64,1024]{2,1,0:T(8,128)(2,1)S(1)}, bf16[1,64,1024]{2,1,0:T(8,128)(2,1)}, u32[]{:S(2)}) copy-start(bf16[1,64,1024]{2,1,0:T(8,128)(2,1)} %param.8) | copy-start | bytes 393220
  30.6 13.5 %collective-permute-start.3 = (f32[64,1024]{1,0:T(8,128)S(1)}, f32[64,1024]{1,0:T(8,128)S(1)}, u32[]{:S(2)}, u32[]{:S(2)}) collective-permute-start(f32[64,1024]{1,0:T(8,128)S(1)} %slice_select_fusion.3), channel_id=1, source_target_pairs={{0,8},{1,9},{2,10},{3,11},{4,12},{5,13},{6,14},{7,15},{8,0},{9,1},... | collective-permute-start | bytes 786440 | tf_op jit(solution)/shard_map/ppermute | solution.py:13
  44.3 1.2 collective-permute-start.5
  45.5 3.5 %collective-permute-start.6 = (f32[64]{0:T(128)S(1)}, f32[64]{0:T(128)S(1)}, u32[]{:S(2)}, u32[]{:S(2)}) collective-permute-start(f32[64]{0:T(128)S(1)} %add.55), channel_id=1, source_target_pairs={{0,2},{1,3},{2,0},{3,1},{4,6},{5,7},{6,4},{7,5},{8,10},{9,11},{10,... | collective-permute-start | bytes 776 | tf_op jit(solution)/shard_map/ppermute | solution.py:13
  49.0 3.5 %collective-permute-start.7 = (f32[64]{0:T(128)S(1)}, f32[64]{0:T(128)S(1)}, u32[]{:S(2)}, u32[]{:S(2)}) collective-permute-start(f32[64]{0:T(128)S(1)} %add.56), channel_id=1, source_target_pairs={{0,4},{1,5},{2,6},{3,7},{4,0},{5,1},{6,2},{7,3},{8,12},{9,13},{10,... | collective-permute-start | bytes 776 | tf_op jit(solution)/shard_map/ppermute | solution.py:13
  52.7 7.3 %collective-permute-start.8 = (bf16[64,1024]{1,0:T(8,128)(2,1)S(1)}, bf16[64,1024]{1,0:T(8,128)(2,1)S(1)}, u32[]{:S(2)}, u32[]{:S(2)}) collective-permute-start(bf16[64,1024]{1,0:T(8,128)(2,1)S(1)} %fusion.31), channel_id=1, source_target_pairs={{0,8},{1,9},{2,10},{3,11},{4,12},{5,13},{6,14},{7,15},{8,0},{9,1},... | collective-permute-start | bytes 393224 | tf_op jit(solution)/shard_map/ppermute | solution.py:13
  75.1 78.1 %collective-permute-start.9 = (f32[2,64,7168]{2,1,0:T(8,128)S(1)}, f32[2,64,7168]{2,1,0:T(8,128)S(1)}, u32[]{:S(2)}, u32[]{:S(2)}) collective-permute-start(f32[2,64,7168]{2,1,0:T(8,128)S(1)} %broadcast_select_fusion), channel_id=1, source_target_pairs={{0,4},{1,5},{2,6},{3,7},{4,0},{5,1},{6,2},{7,3},{8,12},{9,13},{10,... | collective-permute-start | bytes 11010056 | tf_op jit(solution)/shard_map/ppermute | solution.py:13
  153.2 78.1 %slice-start = ((s8[14680064]{0:T(1024)(128)(4,1)}), s8[4194304]{0:T(1024)(128)(4,1)S(1)}, s32[]{:S(2)}) async-start(s8[14680064]{0:T(1024)(128)(4,1)} %bitcast.36), calls=%async_computation | async-start | bytes 8388608
  153.2 78.1 %slice-start.1 = ((s8[14680064]{0:T(1024)(128)(4,1)}), s8[2097152]{0:T(1024)(128)(4,1)S(1)}, s32[]{:S(2)}) async-start(s8[14680064]{0:T(1024)(128)(4,1)} %bitcast.36), calls=%async_computation.1 | async-start | bytes 4194304
  153.9 77.3 %slice-start.2 = ((s8[14680064]{0:T(1024)(128)(4,1)}), s8[4194304]{0:T(1024)(128)(4,1)S(1)}, s32[]{:S(2)}) async-start(s8[14680064]{0:T(1024)(128)(4,1)} %bitcast.36), calls=%async_computation.2 | async-start | bytes 8388608
  154.1 37.8 %collective-permute-start.10 = (f32[2,32,7168]{2,1,0:T(8,128)S(1)}, f32[2,32,7168]{2,1,0:T(8,128)S(1)}, u32[]{:S(2)}, u32[]{:S(2)}) collective-permute-start(f32[2,32,7168]{2,1,0:T(8,128)S(1)} %slice_select_fusion), channel_id=1, source_target_pairs={{0,2},{1,3},{2,0},{3,1},{4,6},{5,7},{6,4},{7,5},{8,10},{9,11},{10,... | collective-permute-start | bytes 5505032 | tf_op jit(solution)/shard_map/ppermute | solution.py:13
  192.2 39.0 %slice-start.3 = ((s8[14680064]{0:T(1024)(128)(4,1)}), s8[4194304]{0:T(1024)(128)(4,1)S(1)}, s32[]{:S(2)}) async-start(s8[14680064]{0:T(1024)(128)(4,1)} %bitcast.36), calls=%async_computation.3 | async-start | bytes 8388608
  192.3 2.5 %collective-permute-start.11 = (f32[2,16,7168]{2,1,0:T(8,128)S(1)}, f32[2,16,7168]{2,1,0:T(8,128)S(1)}, u32[]{:S(2)}, u32[]{:S(2)}) collective-permute-start(f32[2,16,7168]{2,1,0:T(8,128)S(1)} %slice_select_fusion.1), channel_id=1, source_target_pairs={{0,1},{1,0},{2,3},{3,2},{4,5},{5,4},{6,7},{7,6},{8,9},{9,8},{10,11... | collective-permute-start | bytes 2752520 | tf_op jit(solution)/shard_map/ppermute | solution.py:13
  195.2 1.6 collective-permute-start.12
  196.8 12.6 %collective-permute-start.13 = (bf16[32,7168]{1,0:T(8,128)(2,1)S(1)}, bf16[32,7168]{1,0:T(8,128)(2,1)S(1)}, u32[]{:S(2)}, u32[]{:S(2)}) collective-permute-start(bf16[32,7168]{1,0:T(8,128)(2,1)S(1)} %maximum_select_fusion.6), channel_id=1, source_target_pairs={{0,2},{1,3},{2,0},{3,1},{4,6},{5,7},{6,4},{7,5},{8,10},{9,11},{10,... | collective-permute-start | bytes 1376264 | tf_op jit(solution)/shard_map/ppermute | solution.py:13
  209.6 21.6 %collective-permute-start.14 = (bf16[64,7168]{1,0:T(8,128)(2,1)S(1)}, bf16[64,7168]{1,0:T(8,128)(2,1)S(1)}, u32[]{:S(2)}, u32[]{:S(2)}) collective-permute-start(bf16[64,7168]{1,0:T(8,128)(2,1)S(1)} %maximum_select_fusion.4), channel_id=1, source_target_pairs={{0,4},{1,5},{2,6},{3,7},{4,0},{5,1},{6,2},{7,3},{8,12},{9,13},{10,... | collective-permute-start | bytes 2752520 | tf_op jit(solution)/shard_map/ppermute | solution.py:13
  233.5 18.8 %collective-permute-start.15 = (f32[128,512]{1,0:T(8,128)S(1)}, f32[128,512]{1,0:T(8,128)S(1)}, u32[]{:S(2)}, u32[]{:S(2)}) collective-permute-start(f32[128,512]{1,0:T(8,128)S(1)} %slice_select_fusion.2), channel_id=1, source_target_pairs={{0,8},{1,9},{2,10},{3,11},{4,12},{5,13},{6,14},{7,15},{8,0},{9,1},... | collective-permute-start | bytes 786440 | tf_op jit(solution)/shard_map/ppermute | solution.py:13
  235.7 16.6 %collective-permute-start.4 = (bf16[64,1024]{1,0:T(8,128)(2,1)S(1)}, bf16[64,1024]{1,0:T(8,128)(2,1)S(1)}, u32[]{:S(2)}, u32[]{:S(2)}) collective-permute-start(bf16[64,1024]{1,0:T(8,128)(2,1)S(1)} %get-tuple-element.6), channel_id=1, source_target_pairs={{0,8},{1,9},{2,10},{3,11},{4,12},{5,13},{6,14},{7,15},{8,0},{9,1},... | collective-permute-start | bytes 393224 | tf_op jit(solution)/shard_map/ppermute | solution.py:13
where the time goes:
time: 253 us
  waiting for transfers between devices  209 us (83%)
  matrix products  21.3 us (8%)
  starting transfers between devices  17.2 us (7%)
  other arithmetic  4.66 us (2%)
    ppermute x16, waiting for transfers between devices, from_partner(): return lax.ppermute(value, axis, pairs)  209 us
    ppermute x16, starting transfers between devices, from_partner(): return lax.ppermute(value, axis, pairs)  17.2 us
    dot_general x1, matrix products, local(): jnp.dot(token_rows, up_weight[0], preferred_element_type=jnp.float32)  7.26 us
    dot_general x1, matrix products, local(): jnp.dot(token_rows, gate_weight[0], preferred_element_type=jnp.float32)  7.25 us
  transfers between devices with their start and end apart: 16, of which 15 were waited for; matrix products, arithmetic and copies ran while one was open for 0% of the time, Pallas kernels for 0%

commit v1 on v0

--- a/solution.py
+++ b/solution.py
@@ -1,6 +1,10 @@
+import functools
+
 import jax
 import jax.numpy as jnp
 from jax import lax
+from jax.experimental import pallas as pl
+from jax.experimental.pallas import tpu as pltpu
 from jax.sharding import PartitionSpec as P
 
 D = 8192
@@ -120,6 +124,312 @@
     return result[:, None, :]
 
 
+BF = jnp.bfloat16
+F32 = jnp.float32
+CORE, XNBR, ZNBR, OTHER = 1, 2, 4, 8
+PAIRS = 4
+
+
+def grid_kernel(
+    attn, resid, wo, gain, wg, wu, wd, out,
+    wgb, wub, wdb, panel, resb, gainb, pbuf, psend, precv, stream, xb, acc,
+    sq_out, sq_in, scale, keep, send1, recv1, send2, recv2, send3, recv3, hb,
+    dsend, drecv, lsem, ssem, rsem,
+):
+    idx = lax.axis_index("row")
+    core, xpos, zpos, gr = idx % 2, idx // 2 % 2, idx // 4 % 2, idx // 8
+    bits = (core, xpos, zpos, gr)
+    toks, width = pbuf.shape
+    blk = toks // 8
+    half = toks // 2
+    feat = panel.shape[2]
+    wide = wgb.shape[1] // PAIRS
+    sub = wide // 2
+    out_w = width // 2
+
+    def peer(mask):
+        moved = idx
+        for pos, bit in enumerate(bits):
+            if mask >> pos & 1:
+                moved = moved + (1 - 2 * bit) * 2**pos
+        return moved
+
+    def token_block(k):
+        flip = lambda bit, on: 1 - bit if on else bit
+        block = flip(core, k >> 2 & 1) * 4 + flip(xpos, k >> 1 & 1) * 2 + flip(zpos, k & 1)
+        return pl.multiple_of(block * blk, blk)
+
+    count = [0]
+    sent = []
+    local_count = [0]
+
+    def push(src, dst, mask):
+        n = count[0]
+        count[0] += 1
+        copy = pltpu.make_async_remote_copy(
+            src_ref=src, dst_ref=dst, send_sem=ssem.at[n], recv_sem=rsem.at[n],
+            device_id={"row": peer(mask)}, device_id_type=pl.DeviceIdType.MESH,
+        )
+        copy.start()
+        sent.append(copy)
+        return copy
+
+    def fetch(src, dst):
+        n = local_count[0]
+        local_count[0] += 1
+        copy = pltpu.make_async_copy(src, dst, lsem.at[n])
+        copy.start()
+        return copy
+
+    own_load = fetch(attn, panel.at[0])
+    wo_load = {}
+    for d in (0, 2, 4, 1, 3, 5, 6, 7):
+        first = pl.multiple_of((peer(d) - gr * 8) * feat, feat)
+        wo_load[d] = fetch(wo.at[0, pl.ds(first, feat), :], wdb.at[d * feat : (d + 1) * feat])
+    res_load = fetch(resid.at[0], resb)
+    gain_load = fetch(gain.at[pl.ds(pl.multiple_of(idx % 8 * 8, 8), 8), :], gainb)
+
+    barrier = pltpu.get_barrier_semaphore()
+    for mask in (1, 2, 3, 4, 5, 6, 7, 8):
+        pl.semaphore_signal(
+            barrier, inc=1, device_id={"row": peer(mask)}, device_id_type=pl.DeviceIdType.MESH
+        )
+    pl.semaphore_wait(barrier, 8)
+
+    from_x = push(attn, panel.at[XNBR], XNBR)
+    from_z = push(attn, panel.at[ZNBR], ZNBR)
+    from_core = push(attn, panel.at[CORE], CORE)
+
+    def project(d):
+        return jnp.dot(
+            panel[d], wdb[d * feat : (d + 1) * feat, :], preferred_element_type=F32
+        )
+
+    own_load.wait()
+    wo_load[0].wait()
+    pbuf[...] = project(0)
+    from_x.wait_recv()
+    diag_z = push(panel.at[2, 0:half], panel.at[6, 0:half], ZNBR)
+    core_x = push(panel.at[2], panel.at[3], CORE)
+    from_z.wait_recv()
+    diag_x = push(panel.at[4, half:toks], panel.at[6, half:toks], XNBR)
+    core_z = push(panel.at[4], panel.at[5], CORE)
+    for d in (1, 2, 4, 3, 5, 6, 7):
+        wo_load[d].wait()
+    gate_load, up_load = [], []
+    for p in range(PAIRS):
+        cols = slice(p * wide, (p + 1) * wide)
+        gate_load.append(fetch(wg.at[0, :, cols], wgb.at[:, cols]))
+        up_load.append(fetch(wu.at[0, :, cols], wub.at[:, cols]))
+    pbuf[...] += project(2)
+    pbuf[...] += project(4)
+    from_core.wait_recv()
+    pbuf[...] += project(1)
+    diag_z.wait_recv()
+    diag_x.wait_recv()
+    core_d = push(panel.at[6], panel.at[7], CORE)
+    pbuf[...] += project(6)
+    core_x.wait_recv()
+    pbuf[...] += project(3)
+    core_z.wait_recv()
+    pbuf[...] += project(5)
+    core_d.wait_recv()
+    pbuf[...] += project(7)
+
+    res_load.wait()
+    mine = pl.ds(pl.multiple_of(gr * half, half), half)
+    pbuf[mine, :] += resb[...].astype(F32)
+    psend[...] = pbuf[...].astype(BF)
+    from_other = push(psend, precv, OTHER)
+    down_load = []
+    for p in range(PAIRS):
+        rows = slice(p * wide, (p + 1) * wide)
+        both = []
+        for side, owner in ((0, gr), (1, 1 - gr)):
+            first = pl.multiple_of(owner * out_w, out_w)
+            both.append(
+                fetch(
+                    wd.at[0, rows, pl.ds(first, out_w)],
+                    wdb.at[rows, side * out_w : (side + 1) * out_w],
+                )
+            )
+        down_load.append(both)
+    gain_load.wait()
+    gain_row = jnp.concatenate([gainb[j : j + 1, :] for j in range(8)], axis=1)
+    from_other.wait_recv()
+    pbuf[...] += precv[...].astype(F32)
+    for k in range(8):
+        value = pbuf[pl.ds(token_block(k), blk), :]
+        stream[k * blk : (k + 1) * blk, :] = value
+        xb[k * blk : (k + 1) * blk, :] = (value * gain_row).astype(BF)
+
+    sq_copies = []
+
+    def send_squares():
+        total = pbuf[...]
+        total = jnp.sum(total * total, axis=1, keepdims=True)
+        sq_out[...] = jnp.transpose(jnp.broadcast_to(total, (toks, toks)))[0:8, :]
+        for mask in range(1, 8):
+            sq_copies.append(push(sq_out, sq_in.at[mask - 1], mask))
+
+    def make_scale():
+        total = sq_out[...]
+        for copy in sq_copies:
+            copy.wait_recv()
+        for k in range(7):
+            total = total + sq_in[k]
+        spread = jnp.transpose(jnp.broadcast_to(total[0:1, :], (toks, toks)))
+        scale[...] = lax.rsqrt(spread / D + 1e-05)
+
+    state = {}
+
+    def multiply(p):
+        cols = slice(p * wide, (p + 1) * wide)
+        for which, (load, weight) in enumerate(((gate_load, wgb), (up_load, wub))):
+            load[p].wait()
+            value = jnp.dot(xb[...], weight[:, cols], preferred_element_type=F32)
+            for part in range(2):
+                to = slice((2 * part + which) * sub, (2 * part + which + 1) * sub)
+                at = slice(part * sub, (part + 1) * sub)
+                keep[p, :, to] = value[0:half, at]
+                send1[p, :, to] = value[half:toks, at].astype(BF)
+        state["core", p] = push(send1.at[p], recv1.at[p], CORE)
+
+    def fold_core(p):
+        state["core", p].wait_recv()
+        a, b = slice(0, wide), slice(wide, 2 * wide)
+        two = 2 * blk
+
+        def total(rows, cols):
+            return keep[p, rows, cols] + recv1[p, rows, cols].astype(F32)
+
+        send2[p, :, a] = total(slice(two, 2 * two), a).astype(BF)
+        state["a2", p] = push(send2.at[p, :, a], recv2.at[p, :, a], XNBR)
+        send2[p, 0:blk, b] = total(slice(blk, two), b).astype(BF)
+        send2[p, blk:two, b] = total(slice(3 * blk, 4 * blk), b).astype(BF)
+        state["b2", p] = push(send2.at[p, :, b], recv2.at[p, :, b], ZNBR)
+        keep[p, 0:two, a] = total(slice(0, two), a)
+        keep[p, 0:blk, b] = total(slice(0, blk), b)
+        keep[p, two : 3 * blk, b] = total(slice(two, 3 * blk), b)
+
+    def fold_second(p):
+        a, b = slice(0, wide), slice(wide, 2 * wide)
+        two = 2 * blk
+        state["a2", p].wait_recv()
+        send3[p, :, a] = (keep[p, blk:two, a] + recv2[p, blk:two, a].astype(F32)).astype(BF)
+        state["a3", p] = push(send3.at[p, :, a], recv3.at[p, :, a], ZNBR)
+        keep[p, 0:blk, a] += recv2[p, 0:blk, a].astype(F32)
+        state["b2", p].wait_recv()
+        send3[p, :, b] = (
+            keep[p, two : 3 * blk, b] + recv2[p, blk:two, b].astype(F32)
+        ).astype(BF)
+        state["b3", p] = push(send3.at[p, :, b], recv3.at[p, :, b], XNBR)
+        keep[p, 0:blk, b] += recv2[p, 0:blk, b].astype(F32)
+
+    def activate(p):
+        if p == 0:
+            make_scale()
+        factor = scale[pl.ds(token_block(0), blk), 0:1]
+        for part, name in enumerate(("a3", "b3")):
+            state[name, p].wait_recv()
+            gates = slice(2 * part * sub, (2 * part + 1) * sub)
+            ups = slice((2 * part + 1) * sub, (2 * part + 2) * sub)
+            gate = (keep[p, 0:blk, gates] + recv3[p, :, gates].astype(F32)) * factor
+            up = (keep[p, 0:blk, ups] + recv3[p, :, ups].astype(F32)) * factor
+            hidden = gate / (1.0 + jnp.exp(-gate)) * up
+            hb[p, 0:blk, part * sub : (part + 1) * sub] = hidden.astype(BF)
+        state["hz", p] = push(hb.at[p, 0:blk], hb.at[p, blk : 2 * blk], ZNBR)
+        state["hx", p] = push(hb.at[p, 0:blk], hb.at[p, 2 * blk : 3 * blk], XNBR)
+
+    def relay(p):
+        first, last = slice(0, sub), slice(sub, wide)
+        far = slice(3 * blk, 4 * blk)
+        state["hz", p].wait_recv()
+        state["fx", p] = push(hb.at[p, blk : 2 * blk, first], hb.at[p, far, first], XNBR)
+        state["hx", p].wait_recv()
+        state["fz", p] = push(hb.at[p, 2 * blk : 3 * blk, last], hb.at[p, far, last], ZNBR)
+
+    def share_core(p):
+        state["fx", p].wait_recv()
+        state["fz", p].wait_recv()
+        state["hc", p] = push(hb.at[p, 0:half], hb.at[p, half:toks], CORE)
+
+    def down(p):
+        state["hc", p].wait_recv()
+        rows = slice(p * wide, (p + 1) * wide)
+        for side in (1, 0):
+            cols = slice(side * out_w, (side + 1) * out_w)
+            down_load[p][side].wait()
+            value = jnp.dot(hb[p], wdb[rows, cols], preferred_element_type=F32)
+            if p > 0:
+                value = acc[:, cols] + value
+            if p == PAIRS - 1 and side == 1:
+                dsend[...] = value.astype(BF)
+                state["down"] = push(dsend, drecv, OTHER)
+            else:
+                acc[:, cols] = value
+
+    steps = (multiply, fold_core, fold_second, activate, relay, share_core, down)
+    lag = (0, 1, 3, 4, 5, 6, 7)
+    for tick in range(PAIRS + lag[-1]):
+        for step, behind in zip(steps, lag):
+            p = tick - behind
+            if 0 <= p < PAIRS:
+                step(p)
+        if tick == 0:
+            send_squares()
+
+    state["down"].wait_recv()
+    own_cols = pl.ds(pl.multiple_of(gr * out_w, out_w), out_w)
+    for k in range(8):
+        rows = slice(k * blk, (k + 1) * blk)
+        value = stream[rows, own_cols] + acc[rows, 0:out_w] + drecv[rows, :].astype(F32)
+        out[pl.ds(token_block(k), blk), :] = value.astype(BF)
+    for copy in sent:
+        copy.wait_send()
+
+
+def fused(attn_out, residual_in, out_weight, norm_gain, gate_weight, up_weight, down_weight):
+    toks, feat = attn_out.shape
+    width = out_weight.shape[2]
+    ff = gate_weight.shape[2]
+    wide = ff // PAIRS
+    half, blk = toks // 2, toks // 8
+    vm = pltpu.VMEM
+    scratch = [
+        vm((width, ff), BF), vm((width, ff), BF), vm((ff, width), BF),
+        vm((8, toks, feat), BF), vm((half, width), BF), vm((8, 128), F32),
+        vm((toks, width), F32), vm((toks, width), BF), vm((toks, width), BF),
+        vm((toks, width), F32), vm((toks, width), BF), vm((toks, width), F32),
+        vm((8, toks), F32), vm((7, 8, toks), F32), vm((toks, toks), F32),
+        vm((PAIRS, half, 2 * wide), F32),
+        vm((PAIRS, half, 2 * wide), BF), vm((PAIRS, half, 2 * wide), BF),
+        vm((PAIRS, 2 * blk, 2 * wide), BF), vm((PAIRS, 2 * blk, 2 * wide), BF),
+        vm((PAIRS, blk, 2 * wide), BF), vm((PAIRS, blk, 2 * wide), BF),
+        vm((PAIRS, toks, wide), BF),
+        vm((toks, width // 2), BF), vm((toks, width // 2), BF),
+        pltpu.SemaphoreType.DMA((40,)),
+        pltpu.SemaphoreType.DMA((80,)), pltpu.SemaphoreType.DMA((80,)),
+    ]
+    flops = 2 * toks * width * (8 * feat + 3 * ff)
+    traffic = 2 * width * (8 * feat + 3 * ff)
+    result = pl.pallas_call(
+        grid_kernel,
+        out_shape=jax.ShapeDtypeStruct((toks, width // 2), BF),
+        in_specs=[pl.BlockSpec(memory_space=pl.ANY)] * 7,
+        out_specs=pl.BlockSpec(memory_space=pltpu.VMEM),
+        scratch_shapes=scratch,
+        compiler_params=pltpu.CompilerParams(
+            collective_id=0, has_side_effects=True, vmem_limit_bytes=62 * 2**20
+        ),
+        cost_estimate=pl.CostEstimate(flops=flops, bytes_accessed=traffic, transcendentals=0),
+    )(
+        attn_out, residual_in, out_weight, norm_gain.reshape(-1, 128),
+        gate_weight, up_weight, down_weight,
+    )
+    return result[:, None, :]
+
+
 def solution(mesh):
     in_specs = (
         P("groups", "row"),
@@ -131,4 +441,5 @@
         P("row", None, None),
     )
     out_specs = P("groups", "row", None)
-    return jax.shard_map(local, mesh=mesh, in_specs=in_specs, out_specs=out_specs, check_vma=False)
+    body = fused if mesh.shape["row"] == 2 * COLG else local
+    return jax.shard_map(body, mesh=mesh, in_specs=in_specs, out_specs=out_specs, check_vma=False)

time: 253 us -> 71.7 us (0.28)
  waiting for transfers between devices: 209 us -> 0 us
  Pallas kernels: 0 us -> 70 us
  matrix products: 21.3 us -> 0 us
  starting transfers between devices: 17.2 us -> 0 us
  other arithmetic: 4.66 us -> 0 us
    ppermute x16 -> x0, waiting for transfers between devices: 209 us -> none  [from_partner(): return lax.ppermute(value, axis, pairs)]
    pallas_call x0 -> x1, Pallas kernels: none -> 70 us  [fused(): pl.pallas_call(grid_kernel, out_shape=jax.ShapeDtypeStruct((toks, width /...]
    dot_general x4 -> x0, matrix products: 21.3 us -> none  [the longest x1 7.26 us: local(): jnp.dot(token_rows, up_weight[0], preferred_element_type=jnp.float32)]
    ppermute x16 -> x0, starting transfers between devices: 17.2 us -> none  [from_partner(): return lax.ppermute(value, axis, pairs)]
  transfers between devices with their start and end apart: 16 -> 0, of which waited for: 15 -> 0; matrix products, arithmetic and copies ran while one was open for 0% -> 0% of each run, Pallas kernels for 0% -> 0%
where the time goes in v1:
time: 71.7 us; the launch traced here: 71.6 us
  Pallas kernels  70 us (98%)
  local copies, waits for them, and re-layouts  1.57 us (2%)
    pallas_call x1, Pallas kernels, fused(): pl.pallas_call(grid_kernel, out_shape=jax.ShapeDtypeStruct((toks, width /...  70 us
    unnamed x1, local copies, waits for them, and re-layouts  1.57 us

profile of v1, /device:TPU:0, one launch (start us, length us, event | category | flops | bytes accessed | tf_op | source)
XLA Modules:
  0.0 71.6 jit_solution(8099838629370485206)
XLA Ops:
  0.0 70.0 %shard_map.73 = bf16[128,512]{1,0:T(8,128)(2,1)} custom-call(bf16[128,512]{1,0:T(8,128)(2,1)} %attn.1, bf16[1,64,1024]{2,1,0:T(8,128)(2,1)} %resid.1, bf16[1,4096,1024]{2,1,0:T(8,128)(2,1)} %wo.1, f32[64,128]{1,0:T(8,128)} %bitcast.3, bf16[1,1024,7168]{2,1,0:T(8,128)(2,1)} %wg.1, bf16[1,1024,7168]{2,1,0:T(8,128)(2,1)} %wu.1, bf16[1,7168,1024]{2,1,0:T(8,128)(2,1)} %wd.1), custom_call_target="tpu_custom_call" | custom-call | flops 6710886400 | bytes 52428800 | tf_op jit(solution)/shard_map/pallas_call | solution.py:416
  70.0 1.6 %copy.9 = bf16[128,1,512]{2,0,1:T(8,128)(2,1)} copy(bf16[128,1,512]{2,0,1:T(8,128)(2,1)} %bitcast.2) | data formatting | bytes 262144

commit v2 on v0

--- a/solution.py
+++ b/solution.py
@@ -1,6 +1,8 @@
 import jax
 import jax.numpy as jnp
 from jax import lax
+from jax.experimental import pallas as pl
+from jax.experimental.pallas import tpu as pltpu
 from jax.sharding import PartitionSpec as P
 
 D = 8192
@@ -120,6 +122,379 @@
     return result[:, None, :]
 
 
+BF = jnp.bfloat16
+F32 = jnp.float32
+CORE, XNBR, ZNBR, OTHER = 1, 2, 4, 8
+BATCHES = 2
+SHARES = (3, 4, 4, 3)
+CHUNKS = len(SHARES)
+
+
+def chunks_of(units):
+    one = units // sum(SHARES)
+    starts = [one * sum(SHARES[:p]) for p in range(CHUNKS)]
+    return [(start, one * share) for start, share in zip(starts, SHARES)]
+
+
+def grid_kernel(
+    attn, resid, wo, gain, wg, wu, wd, out,
+    wgb, wub, wdb, panel, resb, gainb, pbuf, psend, precv, stream, xb, xs, acc,
+    sq_out, sq_in, scale, keep, send1, recv1, send2, recv2, send3, recv3, hb,
+    dsend, drecv, lsem, ssem, rsem,
+):
+    idx = lax.axis_index("row")
+    core, xpos, zpos, gr = idx % 2, idx // 2 % 2, idx // 4 % 2, idx // 8
+    bits = (core, xpos, zpos, gr)
+    toks, width = pbuf.shape
+    half = toks // BATCHES
+    blk = half // 4
+    two = 2 * blk
+    feat = panel.shape[2]
+    units = wgb.shape[2]
+    out_w = width // 2
+    chunks = chunks_of(units)
+    slots = keep.shape[0]
+
+    def peer(mask):
+        moved = idx
+        for pos, bit in enumerate(bits):
+            if mask >> pos & 1:
+                moved = moved + (1 - 2 * bit) * 2**pos
+        return moved
+
+    to_x, to_z = peer(XNBR) - idx, peer(ZNBR) - idx
+    first_peer = idx + to_x + core * (to_z - to_x)
+    second_peer = idx + to_z + core * (to_x - to_z)
+
+    own_block = xpos * 2 + zpos
+    flip_x, flip_z = 2 * (1 - 2 * xpos), 1 - 2 * zpos
+    block_at = (
+        own_block,
+        own_block + flip_z + core * (flip_x - flip_z),
+        own_block + flip_x + core * (flip_z - flip_x),
+        own_block + flip_x + flip_z,
+    )
+    sibling_order = (0, 2, 1, 3)
+
+    def token_rows(t, k):
+        return pl.ds(pl.multiple_of(t * half + block_at[k] * blk, blk), blk)
+
+    count = [0]
+    sent = []
+    local_count = [0]
+
+    def push_to(src, dst, device):
+        n = count[0]
+        count[0] += 1
+        copy = pltpu.make_async_remote_copy(
+            src_ref=src, dst_ref=dst, send_sem=ssem.at[n], recv_sem=rsem.at[n],
+            device_id={"row": device}, device_id_type=pl.DeviceIdType.MESH,
+        )
+        copy.start()
+        sent.append(copy)
+        return copy
+
+    def push(src, dst, mask):
+        return push_to(src, dst, peer(mask))
+
+    def fetch(src, dst):
+        n = local_count[0]
+        local_count[0] += 1
+        copy = pltpu.make_async_copy(src, dst, lsem.at[n])
+        copy.start()
+        return copy
+
+    own_load = fetch(attn, panel.at[0])
+    wo_load = {}
+    for d in (0, 2, 4, 1, 6, 3, 5, 7):
+        first = pl.multiple_of((peer(d) - gr * 8) * feat, feat)
+        wo_load[d] = fetch(wo.at[0, pl.ds(first, feat), :], wdb.at[d * feat : (d + 1) * feat])
+    res_load = fetch(resid.at[0], resb)
+    gain_load = fetch(gain.at[pl.ds(pl.multiple_of(idx % 8 * 8, 8), 8), :], gainb)
+
+    barrier = pltpu.get_barrier_semaphore()
+    for mask in (1, 2, 3, 4, 5, 6, 7, 8):
+        pl.semaphore_signal(
+            barrier, inc=1, device_id={"row": peer(mask)}, device_id_type=pl.DeviceIdType.MESH
+        )
+    pl.semaphore_wait(barrier, 8)
+
+    from_x = push(attn, panel.at[XNBR], XNBR)
+    from_z = push(attn, panel.at[ZNBR], ZNBR)
+    from_core = push(attn, panel.at[CORE], CORE)
+
+    def project(d):
+        return jnp.dot(
+            panel[d], wdb[d * feat : (d + 1) * feat, :], preferred_element_type=F32
+        )
+
+    own_load.wait()
+    wo_load[0].wait()
+    pbuf[...] = project(0)
+    from_x.wait_recv()
+    mid = toks // 2
+    diag_z = push(panel.at[2, 0:mid], panel.at[6, 0:mid], ZNBR)
+    core_x = push(panel.at[2], panel.at[3], CORE)
+    from_z.wait_recv()
+    diag_x = push(panel.at[4, mid:toks], panel.at[6, mid:toks], XNBR)
+    core_z = push(panel.at[4], panel.at[5], CORE)
+    for d in (1, 2, 4, 3, 5, 6, 7):
+        wo_load[d].wait()
+    gate_load, up_load = [], []
+    for start, sub in chunks:
+        cols = slice(start, start + sub)
+        for loads, weight, buf in ((gate_load, wg, wgb), (up_load, wu, wub)):
+            both = []
+            for side, owner in ((0, core), (1, 1 - core)):
+                first = pl.multiple_of(owner * units + start, 256)
+                both.append(fetch(weight.at[0, :, pl.ds(first, sub)], buf.at[side, :, cols]))
+            loads.append(both)
+    pbuf[...] += project(2)
+    pbuf[...] += project(4)
+    from_core.wait_recv()
+    pbuf[...] += project(1)
+    core_x.wait_recv()
+    pbuf[...] += project(3)
+    diag_z.wait_recv()
+    diag_x.wait_recv()
+    core_d = push(panel.at[6], panel.at[7], CORE)
+    core_z.wait_recv()
+    pbuf[...] += project(5)
+    pbuf[...] += project(6)
+    core_d.wait_recv()
+    pbuf[...] += project(7)
+
+    res_load.wait()
+    mine = pl.ds(pl.multiple_of(gr * mid, mid), mid)
+    pbuf[mine, :] += resb[...].astype(F32)
+    from_other = []
+    for t in range(BATCHES):
+        rows = slice(t * half, (t + 1) * half)
+        psend[rows, :] = pbuf[rows, :].astype(BF)
+        from_other.append(push(psend.at[rows], precv.at[rows], OTHER))
+    down_load = []
+    for start, sub in chunks:
+        both = []
+        for side, owner in ((0, core), (1, 1 - core)):
+            first = pl.multiple_of(owner * units + start, 256)
+            to = 2 * start + side * sub
+            for part, holder in ((0, gr), (1, 1 - gr)):
+                cols = pl.ds(pl.multiple_of(holder * out_w, out_w), out_w)
+                both.append(
+                    fetch(
+                        wd.at[0, pl.ds(first, sub), cols],
+                        wdb.at[to : to + sub, part * out_w : (part + 1) * out_w],
+                    )
+                )
+        down_load.append(both)
+    gain_load.wait()
+    gain_row = jnp.concatenate([gainb[j : j + 1, :] for j in range(8)], axis=1)
+
+    sq_copies = {}
+
+    def receive(t):
+        rows = slice(t * half, (t + 1) * half)
+        from_other[t].wait_recv()
+        pbuf[rows, :] += precv[rows, :].astype(F32)
+        for k in range(4):
+            value = pbuf[token_rows(t, k), :]
+            stream[t * half + k * blk : t * half + (k + 1) * blk, :] = value
+            normed = (value * gain_row).astype(BF)
+            j = sibling_order[k]
+            xb[t * half + k * blk : t * half + (k + 1) * blk, :] = normed
+            xs[t * half + j * blk : t * half + (j + 1) * blk, :] = normed
+
+    def send_squares(t):
+        total = pbuf[t * half : (t + 1) * half, :]
+        total = jnp.sum(total * total, axis=1, keepdims=True)
+        total = jnp.broadcast_to(total, (half, toks))
+        sq_out[t] = jnp.transpose(jnp.concatenate([total] * BATCHES, axis=0))[0:8, :]
+        sq_copies[t] = [
+            push(sq_out.at[t], sq_in.at[t, mask - 1], mask) for mask in range(1, 8)
+        ]
+
+    def make_scale(t):
+        total = sq_out[t]
+        for copy in sq_copies[t]:
+            copy.wait_recv()
+        for k in range(7):
+            total = total + sq_in[t, k]
+        spread = jnp.transpose(jnp.broadcast_to(total[0:1, :], (toks, toks)))
+        scale[t * half : (t + 1) * half, :] = lax.rsqrt(spread[0:half, :] / D + 1e-05)
+
+    state = {}
+
+    def multiply(i):
+        t, p = divmod(i, CHUNKS)
+        start, sub = chunks[p]
+        if p == 0:
+            receive(t)
+        rows = slice(t * half, (t + 1) * half)
+        cols = slice(start, start + sub)
+        for side in (1, 0):
+            for which, (load, weight) in enumerate(((gate_load, wgb), (up_load, wub))):
+                if t == 0:
+                    load[p][side].wait()
+                source = xs if side else xb
+                value = jnp.dot(
+                    source[rows, :], weight[side, :, cols], preferred_element_type=F32
+                )
+                to = slice(which * sub, (which + 1) * sub)
+                if side:
+                    send1[i, :, to] = value.astype(BF)
+                else:
+                    keep[i % slots, :, to] = value
+            if side:
+                both = slice(0, 2 * sub)
+                state["core", i] = push(send1.at[i, :, both], recv1.at[i, :, both], CORE)
+        if p == 0:
+            send_squares(t)
+
+    def fold_core(i):
+        both = slice(0, 2 * chunks[i % CHUNKS][1])
+        state["core", i].wait_recv()
+        s = i % slots
+        send2[i, :, both] = (
+            keep[s, two : 2 * two, both] + recv1[i, two : 2 * two, both].astype(F32)
+        ).astype(BF)
+        state["second", i] = push_to(send2.at[i, :, both], recv2.at[i, :, both], first_peer)
+        keep[s, 0:two, both] += recv1[i, 0:two, both].astype(F32)
+
+    def fold_second(i):
+        both = slice(0, 2 * chunks[i % CHUNKS][1])
+        state["second", i].wait_recv()
+        s = i % slots
+        send3[i, :, both] = (
+            keep[s, blk:two, both] + recv2[i, blk:two, both].astype(F32)
+        ).astype(BF)
+        state["third", i] = push_to(send3.at[i, :, both], recv3.at[i, :, both], second_peer)
+        keep[s, 0:blk, both] += recv2[i, 0:blk, both].astype(F32)
+
+    def share_block(i, k):
+        cols = slice(0, chunks[i % CHUNKS][1])
+        sub = chunks[i % CHUNKS][1]
+        j = sibling_order[k]
+        state["hc", i, k] = push(
+            hb.at[i, k * blk : (k + 1) * blk, cols],
+            hb.at[i, j * blk : (j + 1) * blk, sub : 2 * sub],
+            CORE,
+        )
+
+    def activate(i):
+        t, p = divmod(i, CHUNKS)
+        sub = chunks[p][1]
+        if p == 0:
+            make_scale(t)
+        s = i % slots
+        state["third", i].wait_recv()
+        factor = scale[token_rows(t, 0), 0:1]
+        gate = (keep[s, 0:blk, 0:sub] + recv3[i, :, 0:sub].astype(F32)) * factor
+        up = (keep[s, 0:blk, sub : 2 * sub] + recv3[i, :, sub : 2 * sub].astype(F32)) * factor
+        hb[i, 0:blk, 0:sub] = (gate / (1.0 + jnp.exp(-gate)) * up).astype(BF)
+        own = hb.at[i, 0:blk, 0:sub]
+        state["h1", i] = push_to(own, hb.at[i, blk:two, 0:sub], second_peer)
+        state["h2", i] = push_to(own, hb.at[i, two : 3 * blk, 0:sub], first_peer)
+        share_block(i, 0)
+
+    def relay(i):
+        sub = chunks[i % CHUNKS][1]
+        state["h1", i].wait_recv()
+        state["h3", i] = push_to(
+            hb.at[i, blk:two, 0:sub], hb.at[i, 3 * blk : 4 * blk, 0:sub], first_peer
+        )
+        share_block(i, 1)
+        state["h2", i].wait_recv()
+        share_block(i, 2)
+
+    def share_last(i):
+        state["h3", i].wait_recv()
+        share_block(i, 3)
+
+    def down(i):
+        t, p = divmod(i, CHUNKS)
+        start, sub = chunks[p]
+        for k in range(4):
+            state["hc", i, k].wait_recv()
+        if t == 0:
+            for load in down_load[p]:
+                load.wait()
+        rows = slice(2 * start, 2 * start + 2 * sub)
+        batch = slice(t * half, (t + 1) * half)
+        for part in (1, 0):
+            cols = slice(part * out_w, (part + 1) * out_w)
+            value = jnp.dot(
+                hb[i, :, 0 : 2 * sub], wdb[rows, cols], preferred_element_type=F32
+            )
+            if p > 0:
+                value = acc[batch, cols] + value
+            if p == CHUNKS - 1 and part == 1:
+                dsend[batch, :] = value.astype(BF)
+                state["down", t] = push(dsend.at[batch], drecv.at[batch], OTHER)
+            else:
+                acc[batch, cols] = value
+
+    steps = (multiply, fold_core, fold_second, activate, relay, share_last, down)
+    items = BATCHES * CHUNKS
+    for tick in range(items + len(steps) - 1):
+        for behind, step in enumerate(steps):
+            if 0 <= tick - behind < items:
+                step(tick - behind)
+
+    own_cols = pl.ds(pl.multiple_of(gr * out_w, out_w), out_w)
+    for t in range(BATCHES):
+        state["down", t].wait_recv()
+        for k in range(4):
+            rows = slice(t * half + k * blk, t * half + (k + 1) * blk)
+            value = stream[rows, own_cols] + acc[rows, 0:out_w] + drecv[rows, :].astype(F32)
+            out[token_rows(t, k), :] = value.astype(BF)
+    for copy in sent:
+        copy.wait_send()
+
+
+def fused(attn_out, residual_in, out_weight, norm_gain, gate_weight, up_weight, down_weight):
+    toks, feat = attn_out.shape
+    width = out_weight.shape[2]
+    ff = gate_weight.shape[2]
+    half = toks // BATCHES
+    blk = half // 4
+    items = BATCHES * CHUNKS
+    most = 2 * max(sub for start, sub in chunks_of(ff // 2))
+    vm = pltpu.VMEM
+    scratch = [
+        vm((2, width, ff // 2), BF), vm((2, width, ff // 2), BF), vm((ff, width), BF),
+        vm((8, toks, feat), BF), vm((toks // 2, width), BF), vm((8, 128), F32),
+        vm((toks, width), F32), vm((toks, width), BF), vm((toks, width), BF),
+        vm((toks, width), F32), vm((toks, width), BF), vm((toks, width), BF),
+        vm((toks, width), F32),
+        vm((BATCHES, 8, toks), F32), vm((BATCHES, 7, 8, toks), F32), vm((toks, toks), F32),
+        vm((4, half, most), F32),
+        vm((items, half, most), BF), vm((items, half, most), BF),
+        vm((items, 2 * blk, most), BF), vm((items, 2 * blk, most), BF),
+        vm((items, blk, most), BF), vm((items, blk, most), BF),
+        vm((items, half, most), BF),
+        vm((toks, width // 2), BF), vm((toks, width // 2), BF),
+        pltpu.SemaphoreType.DMA((64,)),
+        pltpu.SemaphoreType.DMA((128,)), pltpu.SemaphoreType.DMA((128,)),
+    ]
+    flops = 2 * toks * width * (8 * feat + 3 * ff)
+    traffic = 2 * width * (8 * feat + 3 * ff)
+    result = pl.pallas_call(
+        grid_kernel,
+        out_shape=jax.ShapeDtypeStruct((toks, width // 2), BF),
+        in_specs=[pl.BlockSpec(memory_space=pl.ANY)] * 7,
+        out_specs=pl.BlockSpec(memory_space=pltpu.VMEM),
+        scratch_shapes=scratch,
+        compiler_params=pltpu.CompilerParams(
+            collective_id=0, has_side_effects=True, vmem_limit_bytes=62 * 2**20
+        ),
+        cost_estimate=pl.CostEstimate(flops=flops, bytes_accessed=traffic, transcendentals=0),
+    )(
+        attn_out, residual_in, out_weight, norm_gain.reshape(-1, 128),
+        gate_weight, up_weight, down_weight,
+    )
+    return result[:, None, :]
+
+
 def solution(mesh):
     in_specs = (
         P("groups", "row"),
@@ -131,4 +506,5 @@
         P("row", None, None),
     )
     out_specs = P("groups", "row", None)
-    return jax.shard_map(local, mesh=mesh, in_specs=in_specs, out_specs=out_specs, check_vma=False)
+    body = fused if mesh.shape["row"] == 2 * COLG else local
+    return jax.shard_map(body, mesh=mesh, in_specs=in_specs, out_specs=out_specs, check_vma=False)

time: 253 us -> 75.9 us (0.30)
  waiting for transfers between devices: 209 us -> 0 us
  Pallas kernels: 0 us -> 74.2 us
  matrix products: 21.3 us -> 0 us
  starting transfers between devices: 17.2 us -> 0 us
  other arithmetic: 4.66 us -> 0 us
    ppermute x16 -> x0, waiting for transfers between devices: 209 us -> none  [from_partner(): return lax.ppermute(value, axis, pairs)]
    pallas_call x0 -> x1, Pallas kernels: none -> 74.2 us  [fused(): pl.pallas_call(grid_kernel, out_shape=jax.ShapeDtypeStruct((toks, width /...]
    dot_general x4 -> x0, matrix products: 21.3 us -> none  [the longest x1 7.26 us: local(): jnp.dot(token_rows, up_weight[0], preferred_element_type=jnp.float32)]
    ppermute x16 -> x0, starting transfers between devices: 17.2 us -> none  [from_partner(): return lax.ppermute(value, axis, pairs)]
  transfers between devices with their start and end apart: 16 -> 0, of which waited for: 15 -> 0; matrix products, arithmetic and copies ran while one was open for 0% -> 0% of each run, Pallas kernels for 0% -> 0%
where the time goes in v2:
time: 75.9 us; the launch traced here: 75.8 us
  Pallas kernels  74.2 us (98%)
  local copies, waits for them, and re-layouts  1.57 us (2%)
    pallas_call x1, Pallas kernels, fused(): pl.pallas_call(grid_kernel, out_shape=jax.ShapeDtypeStruct((toks, width /...  74.2 us
    unnamed x1, local copies, waits for them, and re-layouts  1.57 us

profile of v2, /device:TPU:0, one launch (start us, length us, event | category | flops | bytes accessed | tf_op | source)
XLA Modules:
  0.0 75.8 jit_solution(3970153248420276713)
XLA Ops:
  0.0 74.2 %shard_map.73 = bf16[128,512]{1,0:T(8,128)(2,1)} custom-call(bf16[128,512]{1,0:T(8,128)(2,1)} %attn.1, bf16[1,64,1024]{2,1,0:T(8,128)(2,1)} %resid.1, bf16[1,4096,1024]{2,1,0:T(8,128)(2,1)} %wo.1, f32[64,128]{1,0:T(8,128)} %bitcast.3, bf16[1,1024,7168]{2,1,0:T(8,128)(2,1)} %wg.1, bf16[1,1024,7168]{2,1,0:T(8,128)(2,1)} %wu.1, bf16[1,7168,1024]{2,1,0:T(8,128)(2,1)} %wd.1), custom_call_target="tpu_custom_call" | custom-call | flops 6710886400 | bytes 52428800 | tf_op jit(solution)/shard_map/pallas_call | solution.py:481
  74.2 1.6 %copy.9 = bf16[128,1,512]{2,0,1:T(8,128)(2,1)} copy(bf16[128,1,512]{2,0,1:T(8,128)(2,1)} %bitcast.2) | data formatting | bytes 262144

commit v3 on v2

v3 whole, which is shorter than its diff:
```python
import jax
import jax.numpy as jnp
from jax import lax
from jax.experimental import pallas as pl
from jax.experimental.pallas import tpu as pltpu
from jax.sharding import PartitionSpec as P

D = 8192
COLG = 8


def from_partner(value, axis, stride):
    mask = 2**stride
    pairs = [(source, source ^ mask) for source in range(lax.axis_size(axis))]
    return lax.ppermute(value, axis, pairs)


def gather_bits(value, dim, bit_list, device_pos, sender):
    for bit_pos in bit_list:
        incoming = sender(value, bit_pos)
        on_low = device_pos >> bit_pos & 1 == 0
        value = jnp.where(
            on_low, jnp.concatenate([value, incoming], dim), jnp.concatenate([incoming, value], dim)
        )
    return value


def reduce_bits(value, dim, bit_list, device_pos, sender):
    for bit_pos in reversed(bit_list):
        middle = value.shape[dim] // 2
        bottom = lax.slice_in_dim(value, 0, middle, axis=dim)
        top_part = lax.slice_in_dim(value, middle, 2 * middle, axis=dim)
        on_low = device_pos >> bit_pos & 1 == 0
        kept = jnp.where(on_low, bottom, top_part)
        outgoing = jnp.where(on_low, top_part, bottom)
        value = kept + sender(outgoing, bit_pos)
    return value


def sum_bits(value, bit_list, sender):
    for bit_pos in bit_list:
        value = value + sender(value, bit_pos)
    return value


def local(attn_out, residual_in, out_weight, norm_gain, gate_weight, up_weight, down_weight):
    all_bits = lax.axis_size("row").bit_length() - 1
    col_count = COLG.bit_length() - 1
    col_bits = list(range(col_count))
    row_bits = list(range(col_count, all_bits))
    device_pos = lax.axis_index("row")
    col_index = device_pos % COLG
    row_index = device_pos // COLG
    panel_in = gather_bits(
        attn_out,
        1,
        col_bits,
        device_pos,
        lambda block_piece, bit_pos: from_partner(block_piece, "row", bit_pos),
    )
    partial_proj = jnp.dot(panel_in, out_weight[0], preferred_element_type=jnp.float32)
    projected = reduce_bits(
        partial_proj,
        0,
        row_bits,
        device_pos,
        lambda block_piece, bit_pos: from_partner(block_piece, "row", bit_pos),
    )
    stream = (residual_in[0].astype(jnp.float32) + projected).astype(jnp.bfloat16)
    widened = stream.astype(jnp.float32)
    feat_cols = widened.shape[1]
    squares = jnp.sum(widened * widened, axis=-1)
    squares = sum_bits(
        squares, col_bits, lambda block_piece, bit_pos: from_partner(block_piece, "row", bit_pos)
    )
    mean_square = (squares / D)[:, None]
    gain_part = lax.dynamic_slice_in_dim(norm_gain, col_index * feat_cols, feat_cols)
    normed = (widened * lax.rsqrt(mean_square + 1e-05) * gain_part).astype(jnp.bfloat16)
    token_rows = gather_bits(
        normed,
        0,
        row_bits,
        device_pos,
        lambda block_piece, bit_pos: from_partner(block_piece, "row", bit_pos),
    )
    gate_vals = jnp.dot(token_rows, gate_weight[0], preferred_element_type=jnp.float32)
    up_vals = jnp.dot(token_rows, up_weight[0], preferred_element_type=jnp.float32)
    stacked = jnp.stack([gate_vals, up_vals])
    summed = reduce_bits(
        stacked,
        1,
        col_bits,
        device_pos,
        lambda block_piece, bit_pos: from_partner(block_piece, "row", bit_pos),
    )
    hidden = (jax.nn.silu(summed[0]) * summed[1]).astype(jnp.bfloat16)
    hidden_rows = gather_bits(
        hidden,
        0,
        col_bits,
        device_pos,
        lambda block_piece, bit_pos: from_partner(block_piece, "row", bit_pos),
    )
    partial_down = jnp.dot(hidden_rows, down_weight[0], preferred_element_type=jnp.float32)
    piece_width = feat_cols // 2 ** len(row_bits)
    stream_rows = gather_bits(
        stream,
        0,
        row_bits,
        device_pos,
        lambda block_piece, bit_pos: from_partner(block_piece, "row", bit_pos),
    )
    stream_piece = lax.dynamic_slice_in_dim(stream_rows, row_index * piece_width, piece_width, 1)
    down_piece = reduce_bits(
        partial_down,
        1,
        row_bits,
        device_pos,
        lambda block_piece, bit_pos: from_partner(block_piece, "row", bit_pos),
    )
    result = (stream_piece.astype(jnp.float32) + down_piece).astype(jnp.bfloat16)
    return result[:, None, :]


BF = jnp.bfloat16
F32 = jnp.float32
CORE, XNBR, ZNBR, OTHER = 1, 2, 4, 8
PIECES = 4
SHARES = (4, 4, 4, 2)
CHUNKS = len(SHARES)


def chunks_of(units):
    one = units // sum(SHARES)
    starts = [one * sum(SHARES[:p]) for p in range(CHUNKS)]
    return [(start, one * share) for start, share in zip(starts, SHARES)]


def grid_kernel(
    attn, resid, wo, gain, wg, wu, wd, own_out, other_out,
    wgb, wub, wdb, panel, resb, gainb, pbuf, psend, precv, xb, xs, acc,
    sq_out, sq_in, scale, keep, give, send1, recv1, send2, recv2, send3, recv3, hb,
    dsend, lsem, ssem, rsem,
):
    idx = lax.axis_index("row")
    core, xpos, zpos, gr = idx % 2, idx // 2 % 2, idx // 4 % 2, idx // 8
    bits = (core, xpos, zpos, gr)
    toks, width = pbuf.shape
    blk = toks // 4
    two = 2 * blk
    feat = panel.shape[2]
    units = wgb.shape[2]
    out_w = width // 2
    chunks = chunks_of(units)
    piece = width // PIECES

    def peer(mask):
        moved = idx
        for pos, bit in enumerate(bits):
            if mask >> pos & 1:
                moved = moved + (1 - 2 * bit) * 2**pos
        return moved

    to_x, to_z = peer(XNBR) - idx, peer(ZNBR) - idx
    first_peer = idx + to_x + core * (to_z - to_x)
    second_peer = idx + to_z + core * (to_x - to_z)

    own_block = xpos * 2 + zpos
    flip_x, flip_z = 2 * (1 - 2 * xpos), 1 - 2 * zpos
    block_at = (
        own_block,
        own_block + flip_z + core * (flip_x - flip_z),
        own_block + flip_x + core * (flip_z - flip_x),
        own_block + flip_x + flip_z,
    )
    sibling_order = (0, 2, 1, 3)

    def token_rows(k):
        return pl.ds(pl.multiple_of(block_at[k] * blk, blk), blk)

    def feats(q):
        return slice(q * piece, (q + 1) * piece)

    count = [0]
    sent = []
    local_count = [0]

    def push_to(src, dst, device):
        n = count[0]
        count[0] += 1
        copy = pltpu.make_async_remote_copy(
            src_ref=src, dst_ref=dst, send_sem=ssem.at[n], recv_sem=rsem.at[n],
            device_id={"row": device}, device_id_type=pl.DeviceIdType.MESH,
        )
        copy.start()
        sent.append(copy)
        return copy

    def push(src, dst, mask):
        return push_to(src, dst, peer(mask))

    def fetch(src, dst):
        n = local_count[0]
        local_count[0] += 1
        copy = pltpu.make_async_copy(src, dst, lsem.at[n])
        copy.start()
        return copy

    own_load = fetch(attn, panel.at[0])
    wo_load = {}
    for d in (0, 2, 4, 1, 6, 3, 5, 7):
        first = pl.multiple_of((peer(d) - gr * 8) * feat, feat)
        wo_load[d] = fetch(wo.at[0, pl.ds(first, feat), :], wdb.at[d * feat : (d + 1) * feat])
    res_load = fetch(resid.at[0], resb)
    gain_load = fetch(gain.at[pl.ds(pl.multiple_of(idx % 8 * 8, 8), 8), :], gainb)

    barrier = pltpu.get_barrier_semaphore()
    for mask in (1, 2, 3, 4, 5, 6, 7, 8):
        pl.semaphore_signal(
            barrier, inc=1, device_id={"row": peer(mask)}, device_id_type=pl.DeviceIdType.MESH
        )
    pl.semaphore_wait(barrier, 8)

    gate_up_load = {}

    def load_gate_up(q):
        for which, (weight, buf) in enumerate(((wg, wgb), (wu, wub))):
            for side, owner in ((0, core), (1, 1 - core)):
                cols = pl.ds(pl.multiple_of(owner * units, units), units)
                gate_up_load[q, which, side] = fetch(
                    weight.at[0, feats(q), cols], buf.at[side, feats(q), :]
                )

    from_x = push(attn, panel.at[XNBR], XNBR)
    from_z = push(attn, panel.at[ZNBR], ZNBR)
    from_core = push(attn, panel.at[CORE], CORE)

    def project(d):
        return jnp.dot(
            panel[d], wdb[d * feat : (d + 1) * feat, :], preferred_element_type=F32
        )

    load_gate_up(0)
    own_load.wait()
    wo_load[0].wait()
    pbuf[...] = project(0)
    from_x.wait_recv()
    mid = toks // 2
    diag_z = push(panel.at[2, 0:mid], panel.at[6, 0:mid], ZNBR)
    core_x = push(panel.at[2], panel.at[3], CORE)
    from_z.wait_recv()
    diag_x = push(panel.at[4, mid:toks], panel.at[6, mid:toks], XNBR)
    core_z = push(panel.at[4], panel.at[5], CORE)
    for d in (1, 2, 4, 3, 5, 6, 7):
        wo_load[d].wait()
    for q in range(1, PIECES):
        load_gate_up(q)
    pbuf[...] += project(2)
    pbuf[...] += project(4)
    from_core.wait_recv()
    pbuf[...] += project(1)
    core_x.wait_recv()
    pbuf[...] += project(3)
    diag_z.wait_recv()
    diag_x.wait_recv()
    core_d = push(panel.at[6], panel.at[7], CORE)
    core_z.wait_recv()
    pbuf[...] += project(5)
    pbuf[...] += project(6)
    core_d.wait_recv()

    res_load.wait()
    mine = pl.ds(pl.multiple_of(gr * mid, mid), mid)
    pbuf[mine, :] += resb[...].astype(F32)
    from_other = []
    for q in range(PIECES):
        value = pbuf[:, feats(q)] + jnp.dot(
            panel[7], wdb[7 * feat : 8 * feat, feats(q)], preferred_element_type=F32
        )
        pbuf[:, feats(q)] = value
        psend[:, feats(q)] = value.astype(BF)
        from_other.append(push(psend.at[:, feats(q)], precv.at[:, feats(q)], OTHER))
    down_load = []
    for start, sub in chunks:
        both = []
        for side, owner in ((0, core), (1, 1 - core)):
            first = pl.multiple_of(owner * units + start, 256)
            to = 2 * start + side * sub
            for part, holder in ((0, gr), (1, 1 - gr)):
                cols = pl.ds(pl.multiple_of(holder * out_w, out_w), out_w)
                both.append(
                    fetch(
                        wd.at[0, pl.ds(first, sub), cols],
                        wdb.at[to : to + sub, part * out_w : (part + 1) * out_w],
                    )
                )
        down_load.append(both)
    gain_load.wait()
    gain_row = jnp.concatenate([gainb[j : j + 1, :] for j in range(8)], axis=1)

    sq_copies = []

    def receive(q):
        cols = feats(q)
        from_other[q].wait_recv()
        pbuf[:, cols] += precv[:, cols].astype(F32)
        for k in range(4):
            normed = (pbuf[token_rows(k), cols] * gain_row[:, cols]).astype(BF)
            j = sibling_order[k]
            xb[k * blk : (k + 1) * blk, cols] = normed
            xs[j * blk : (j + 1) * blk, cols] = normed

    def send_squares():
        total = pbuf[...]
        total = jnp.sum(total * total, axis=1, keepdims=True)
        sq_out[...] = jnp.transpose(jnp.broadcast_to(total, (toks, toks)))[0:8, :]
        for mask in range(1, 8):
            sq_copies.append(push(sq_out, sq_in.at[mask - 1], mask))

    def make_scale():
        total = sq_out[...]
        for copy in sq_copies:
            copy.wait_recv()
        for k in range(7):
            total = total + sq_in[k]
        spread = jnp.transpose(jnp.broadcast_to(total[0:1, :], (toks, toks)))
        scale[...] = lax.rsqrt(spread / D + 1e-05)

    state = {}

    def columns(p):
        start, sub = chunks[p]
        return slice(2 * start, 2 * start + 2 * sub)

    def product(p, q, side, which):
        start, sub = chunks[p]
        source, weight = (xs if side else xb), (wub if which else wgb)
        return jnp.dot(
            source[:, feats(q)],
            weight[side, feats(q), start : start + sub],
            preferred_element_type=F32,
        )

    def add_piece(q):
        for p, (start, sub) in enumerate(chunks):
            for side, buf in ((1, give), (0, keep)):
                for which in range(2):
                    if p == 0:
                        gate_up_load[q, which, side].wait()
                    to = slice(2 * start + which * sub, 2 * start + (which + 1) * sub)
                    value = product(p, q, side, which)
                    buf[:, to] = value if q == 0 else buf[:, to] + value

    def multiply(p):
        start, sub = chunks[p]
        q = PIECES - 1
        for side in (1, 0):
            for which in range(2):
                if p == 0:
                    gate_up_load[q, which, side].wait()
                to = slice(2 * start + which * sub, 2 * start + (which + 1) * sub)
                value = product(p, q, side, which)
                if side:
                    send1[:, to] = (give[:, to] + value).astype(BF)
                else:
                    keep[:, to] += value
            if side:
                both = columns(p)
                state["core", p] = push(send1.at[:, both], recv1.at[:, both], CORE)

    def fold_core(p):
        both = columns(p)
        state["core", p].wait_recv()
        send2[:, both] = (
            keep[two : 2 * two, both] + recv1[two : 2 * two, both].astype(F32)
        ).astype(BF)
        state["second", p] = push_to(send2.at[:, both], recv2.at[:, both], first_peer)
        keep[0:two, both] += recv1[0:two, both].astype(F32)

    def fold_second(p):
        both = columns(p)
        state["second", p].wait_recv()
        send3[:, both] = (keep[blk:two, both] + recv2[blk:two, both].astype(F32)).astype(BF)
        state["third", p] = push_to(send3.at[:, both], recv3.at[:, both], second_peer)
        keep[0:blk, both] += recv2[0:blk, both].astype(F32)

    def own_units(p):
        start, sub = chunks[p]
        return slice(2 * start, 2 * start + sub)

    def sibling_units(p):
        start, sub = chunks[p]
        return slice(2 * start + sub, 2 * start + 2 * sub)

    def share_block(p, k):
        j = sibling_order[k]
        state["hc", p, k] = push(
            hb.at[k * blk : (k + 1) * blk, own_units(p)],
            hb.at[j * blk : (j + 1) * blk, sibling_units(p)],
            CORE,
        )

    def activate(p):
        if p == 0:
            make_scale()
        cols, ups = own_units(p), sibling_units(p)
        state["third", p].wait_recv()
        factor = scale[token_rows(0), 0:1]
        gate = (keep[0:blk, cols] + recv3[:, cols].astype(F32)) * factor
        up = (keep[0:blk, ups] + recv3[:, ups].astype(F32)) * factor
        hb[0:blk, cols] = (gate / (1.0 + jnp.exp(-gate)) * up).astype(BF)
        own = hb.at[0:blk, cols]
        state["h1", p] = push_to(own, hb.at[blk:two, cols], second_peer)
        state["h2", p] = push_to(own, hb.at[two : 3 * blk, cols], first_peer)
        share_block(p, 0)

    def relay(p):
        cols = own_units(p)
        state["h1", p].wait_recv()
        state["h3", p] = push_to(
            hb.at[blk:two, cols], hb.at[3 * blk : 4 * blk, cols], first_peer
        )
        share_block(p, 1)
        state["h2", p].wait_recv()
        share_block(p, 2)

    def share_last(p):
        state["h3", p].wait_recv()
        share_block(p, 3)

    def down(p):
        for k in range(4):
            state["hc", p, k].wait_recv()
        for load in down_load[p]:
            load.wait()
        for part in (1, 0):
            cols = slice(part * out_w, (part + 1) * out_w)
            value = jnp.dot(hb[:, columns(p)], wdb[columns(p), cols], preferred_element_type=F32)
            if p > 0:
                value = acc[:, cols] + value
            if p == CHUNKS - 1 and part == 1:
                dsend[...] = value.astype(BF)
                for k in range(4):
                    state["down", k] = push(
                        dsend.at[k * blk : (k + 1) * blk], other_out.at[token_rows(k)], OTHER
                    )
            else:
                acc[:, cols] = value

    for q in range(PIECES - 1):
        receive(q)
        add_piece(q)
    receive(PIECES - 1)
    steps = (multiply, fold_core, fold_second, activate, relay, share_last, down)
    lag = (0, 1, 4, 5, 6, 7, 8)
    for tick in range(CHUNKS + lag[-1]):
        for behind, step in zip(lag, steps):
            if 0 <= tick - behind < CHUNKS:
                step(tick - behind)
        if tick == 1:
            send_squares()

    own_cols = pl.ds(pl.multiple_of(gr * out_w, out_w), out_w)
    for k in range(4):
        rows = slice(k * blk, (k + 1) * blk)
        own_out[token_rows(k), :] = pbuf[token_rows(k), own_cols] + acc[rows, 0:out_w]
    for k in range(4):
        state["down", k].wait_recv()
    for copy in sent:
        copy.wait_send()


def fused(attn_out, residual_in, out_weight, norm_gain, gate_weight, up_weight, down_weight):
    toks, feat = attn_out.shape
    width = out_weight.shape[2]
    ff = gate_weight.shape[2]
    blk = toks // 4
    vm = pltpu.VMEM
    scratch = [
        vm((2, width, ff // 2), BF), vm((2, width, ff // 2), BF), vm((ff, width), BF),
        vm((8, toks, feat), BF), vm((toks // 2, width), BF), vm((8, 128), F32),
        vm((toks, width), F32), vm((toks, width), BF), vm((toks, width), BF),
        vm((toks, width), BF), vm((toks, width), BF), vm((toks, width), F32),
        vm((8, toks), F32), vm((7, 8, toks), F32), vm((toks, toks), F32),
        vm((toks, ff), F32), vm((toks, ff), F32), vm((toks, ff), BF), vm((toks, ff), BF),
        vm((2 * blk, ff), BF), vm((2 * blk, ff), BF),
        vm((blk, ff), BF), vm((blk, ff), BF),
        vm((toks, ff), BF), vm((toks, width // 2), BF),
        pltpu.SemaphoreType.DMA((64,)),
        pltpu.SemaphoreType.DMA((96,)), pltpu.SemaphoreType.DMA((96,)),
    ]
    flops = 2 * toks * width * (8 * feat + 3 * ff)
    traffic = 2 * width * (8 * feat + 3 * ff)
    own, other = pl.pallas_call(
        grid_kernel,
        out_shape=(
            jax.ShapeDtypeStruct((toks, width // 2), F32),
            jax.ShapeDtypeStruct((toks, width // 2), BF),
        ),
        in_specs=[pl.BlockSpec(memory_space=pl.ANY)] * 7,
        out_specs=(
            pl.BlockSpec(memory_space=pltpu.VMEM), pl.BlockSpec(memory_space=pl.ANY)
        ),
        scratch_shapes=scratch,
        compiler_params=pltpu.CompilerParams(
            collective_id=0, has_side_effects=True, vmem_limit_bytes=62 * 2**20
        ),
        cost_estimate=pl.CostEstimate(flops=flops, bytes_accessed=traffic, transcendentals=0),
    )(
        attn_out, residual_in, out_weight, norm_gain.reshape(-1, 128),
        gate_weight, up_weight, down_weight,
    )
    return (own + other.astype(F32)).astype(BF)[:, None, :]


def solution(mesh):
    in_specs = (
        P("groups", "row"),
        P("row", "groups", None),
        P("row", None, None),
        P(),
        P("row", None, None),
        P("row", None, None),
        P("row", None, None),
    )
    out_specs = P("groups", "row", None)
    body = fused if mesh.shape["row"] == 2 * COLG else local
    return jax.shard_map(body, mesh=mesh, in_specs=in_specs, out_specs=out_specs, check_vma=False)
```

time: 75.9 us -> 74.4 us (0.980)
  other arithmetic: 0 us -> 1.67 us
  Pallas kernels: 74.2 us -> 72.6 us
  local copies, waits for them, and re-layouts: 1.57 us -> 0 us
    broadcast_in_dim x0 -> x1, other arithmetic: none -> 1.67 us  [fused(): return (own + other.astype(F32)).astype(BF)[:, None, :]]
    pallas_call x1, Pallas kernels: 74.2 us -> 72.6 us  [fused(): pl.pallas_call(grid_kernel, out_shape=(jax.ShapeDtypeStruct((toks, width...]
    unnamed x1 -> x0, local copies, waits for them, and re-layouts: 1.57 us -> none
where the time goes in v3:
time: 74.4 us; the launch traced here: 74.3 us
  Pallas kernels  72.6 us (98%)
  other arithmetic  1.67 us (2%)
    pallas_call x1, Pallas kernels, fused(): pl.pallas_call(grid_kernel, out_shape=(jax.ShapeDtypeStruct((toks, width...  72.6 us
    broadcast_in_dim x1, other arithmetic, fused(): return (own + other.astype(F32)).astype(BF)[:, None, :]  1.67 us

profile of v3, /device:TPU:0, one launch (start us, length us, event | category | flops | bytes accessed | tf_op | source)
XLA Modules:
  0.0 74.3 jit_solution(12097014381879686586)
XLA Ops:
  0.0 72.6 %shard_map.73 = (f32[128,512]{1,0:T(8,128)}, bf16[128,512]{1,0:T(8,128)(2,1)}) custom-call(bf16[128,512]{1,0:T(8,128)(2,1)} %attn.1, bf16[1,64,1024]{2,1,0:T(8,128)(2,1)} %resid.1, bf16[1,4096,1024]{2,1,0:T(8,128)(2,1)} %wo.1, f32[64,128]{1,0:T(8,128)} %bitcast.3, bf16[1,1024,7168]{2,1,0:T(8,128)(2,1)} %wg.1, bf16[1,1024,7168]{2,1,0:T(8,128)(2,1)} %wu.1, ...), custom_call_target="tpu_custom_call" | custom-call | flops 6710886400 | bytes 52428800 | tf_op jit(solution)/shard_map/pallas_call | solution.py:494
  72.6 1.7 %fusion = bf16[128,1,512]{2,0,1:T(8,128)(2,1)} fusion(f32[128,512]{1,0:T(8,128)} %get-tuple-element.7, bf16[128,512]{1,0:T(8,128)(2,1)} %get-tuple-element.8), kind=kLoop, calls=%fused_computation.1 | loop fusion | flops 196608 | bytes 524288 | tf_op jit(solution)/shard_map/broadcast_in_dim | solution.py:513

commit v4 on v2

--- a/solution.py
+++ b/solution.py
@@ -126,21 +126,29 @@
 F32 = jnp.float32
 CORE, XNBR, ZNBR, OTHER = 1, 2, 4, 8
 BATCHES = 2
-SHARES = (3, 4, 4, 3)
-CHUNKS = len(SHARES)
+SHARES = (3, 4)
+ITEMS = ((0, 0), (0, 1), (1, 1), (1, 0))
 
 
 def chunks_of(units):
     one = units // sum(SHARES)
-    starts = [one * sum(SHARES[:p]) for p in range(CHUNKS)]
-    return [(start, one * share) for start, share in zip(starts, SHARES)]
+    return [(one * sum(SHARES[:p]), one * share) for p, share in enumerate(SHARES)]
+
+
+def columns_of(units):
+    spans, start = [], 0
+    for t, p in ITEMS:
+        wide = 2 * chunks_of(units)[p][1]
+        spans.append(slice(start, start + wide))
+        start += wide
+    return spans
 
 
 def grid_kernel(
-    attn, resid, wo, gain, wg, wu, wd, out,
-    wgb, wub, wdb, panel, resb, gainb, pbuf, psend, precv, stream, xb, xs, acc,
+    attn, resid, wo, gain, wg, wu, wd, own_out, other_out,
+    wgb, wub, wdb, panel, resb, gainb, pbuf, psend, precv, xb, acc,
     sq_out, sq_in, scale, keep, send1, recv1, send2, recv2, send3, recv3, hb,
-    dsend, drecv, lsem, ssem, rsem,
+    dsend, lsem, ssem, rsem,
 ):
     idx = lax.axis_index("row")
     core, xpos, zpos, gr = idx % 2, idx // 2 % 2, idx // 4 % 2, idx // 8
@@ -153,7 +161,7 @@
     units = wgb.shape[2]
     out_w = width // 2
     chunks = chunks_of(units)
-    slots = keep.shape[0]
+    spans = columns_of(units)
 
     def peer(mask):
         moved = idx
@@ -162,40 +170,32 @@
                 moved = moved + (1 - 2 * bit) * 2**pos
         return moved
 
-    to_x, to_z = peer(XNBR) - idx, peer(ZNBR) - idx
-    first_peer = idx + to_x + core * (to_z - to_x)
-    second_peer = idx + to_z + core * (to_x - to_z)
-
     own_block = xpos * 2 + zpos
     flip_x, flip_z = 2 * (1 - 2 * xpos), 1 - 2 * zpos
     block_at = (
-        own_block,
-        own_block + flip_z + core * (flip_x - flip_z),
-        own_block + flip_x + core * (flip_z - flip_x),
-        own_block + flip_x + flip_z,
-    )
-    sibling_order = (0, 2, 1, 3)
+        own_block, own_block + flip_z, own_block + flip_x, own_block + flip_x + flip_z
+    )
 
     def token_rows(t, k):
         return pl.ds(pl.multiple_of(t * half + block_at[k] * blk, blk), blk)
+
+    def batch_rows(t):
+        return slice(t * half, (t + 1) * half)
 
     count = [0]
     sent = []
     local_count = [0]
 
-    def push_to(src, dst, device):
+    def push(src, dst, mask):
         n = count[0]
         count[0] += 1
         copy = pltpu.make_async_remote_copy(
             src_ref=src, dst_ref=dst, send_sem=ssem.at[n], recv_sem=rsem.at[n],
-            device_id={"row": device}, device_id_type=pl.DeviceIdType.MESH,
+            device_id={"row": peer(mask)}, device_id_type=pl.DeviceIdType.MESH,
         )
         copy.start()
         sent.append(copy)
         return copy
-
-    def push(src, dst, mask):
-        return push_to(src, dst, peer(mask))
 
     def fetch(src, dst):
         n = local_count[0]
@@ -219,6 +219,17 @@
         )
     pl.semaphore_wait(barrier, 8)
 
+    gate_up_load = {}
+
+    def load_gate_up(p):
+        start, sub = chunks[p]
+        for which, (weight, buf) in enumerate(((wg, wgb), (wu, wub))):
+            for side, owner in ((1, 1 - core), (0, core)):
+                cols = pl.ds(pl.multiple_of(owner * units + start, 256), sub)
+                gate_up_load[p, which, side] = fetch(
+                    weight.at[0, :, cols], buf.at[side, :, start : start + sub]
+                )
+
     from_x = push(attn, panel.at[XNBR], XNBR)
     from_z = push(attn, panel.at[ZNBR], ZNBR)
     from_core = push(attn, panel.at[CORE], CORE)
@@ -228,6 +239,7 @@
             panel[d], wdb[d * feat : (d + 1) * feat, :], preferred_element_type=F32
         )
 
+    load_gate_up(0)
     own_load.wait()
     wo_load[0].wait()
     pbuf[...] = project(0)
@@ -240,15 +252,8 @@
     core_z = push(panel.at[4], panel.at[5], CORE)
     for d in (1, 2, 4, 3, 5, 6, 7):
         wo_load[d].wait()
-    gate_load, up_load = [], []
-    for start, sub in chunks:
-        cols = slice(start, start + sub)
-        for loads, weight, buf in ((gate_load, wg, wgb), (up_load, wu, wub)):
-            both = []
-            for side, owner in ((0, core), (1, 1 - core)):
-                first = pl.multiple_of(owner * units + start, 256)
-                both.append(fetch(weight.at[0, :, pl.ds(first, sub)], buf.at[side, :, cols]))
-            loads.append(both)
+    for p in range(1, len(chunks)):
+        load_gate_up(p)
     pbuf[...] += project(2)
     pbuf[...] += project(4)
     from_core.wait_recv()
@@ -269,8 +274,10 @@
     pbuf[mine, :] += resb[...].astype(F32)
     from_other = []
     for t in range(BATCHES):
-        rows = slice(t * half, (t + 1) * half)
+        rows = batch_rows(t)
         psend[rows, :] = pbuf[rows, :].astype(BF)
+        if t > 0:
+            sent.pop().wait_send()
         from_other.append(push(psend.at[rows], precv.at[rows], OTHER))
     down_load = []
     for start, sub in chunks:
@@ -293,19 +300,15 @@
     sq_copies = {}
 
     def receive(t):
-        rows = slice(t * half, (t + 1) * half)
+        rows = batch_rows(t)
         from_other[t].wait_recv()
         pbuf[rows, :] += precv[rows, :].astype(F32)
         for k in range(4):
-            value = pbuf[token_rows(t, k), :]
-            stream[t * half + k * blk : t * half + (k + 1) * blk, :] = value
-            normed = (value * gain_row).astype(BF)
-            j = sibling_order[k]
-            xb[t * half + k * blk : t * half + (k + 1) * blk, :] = normed
-            xs[t * half + j * blk : t * half + (j + 1) * blk, :] = normed
+            to = slice(t * half + k * blk, t * half + (k + 1) * blk)
+            xb[to, :] = (pbuf[token_rows(t, k), :] * gain_row).astype(BF)
 
     def send_squares(t):
-        total = pbuf[t * half : (t + 1) * half, :]
+        total = pbuf[batch_rows(t), :]
         total = jnp.sum(total * total, axis=1, keepdims=True)
         total = jnp.broadcast_to(total, (half, toks))
         sq_out[t] = jnp.transpose(jnp.concatenate([total] * BATCHES, axis=0))[0:8, :]
@@ -320,133 +323,155 @@
         for k in range(7):
             total = total + sq_in[t, k]
         spread = jnp.transpose(jnp.broadcast_to(total[0:1, :], (toks, toks)))
-        scale[t * half : (t + 1) * half, :] = lax.rsqrt(spread[0:half, :] / D + 1e-05)
+        scale[batch_rows(t), :] = lax.rsqrt(spread[0:half, :] / D + 1e-05)
 
     state = {}
 
+    def parts(i):
+        span = spans[i]
+        quarter = (span.stop - span.start) // 4
+        edges = [span.start + n * quarter for n in range(5)]
+        return quarter, edges
+
     def multiply(i):
-        t, p = divmod(i, CHUNKS)
+        t, p = ITEMS[i]
         start, sub = chunks[p]
-        if p == 0:
+        quarter, edges = parts(i)
+        if i == 0 or ITEMS[i - 1][0] != t:
             receive(t)
-        rows = slice(t * half, (t + 1) * half)
-        cols = slice(start, start + sub)
         for side in (1, 0):
-            for which, (load, weight) in enumerate(((gate_load, wgb), (up_load, wub))):
+            for which, weight in enumerate((wgb, wub)):
                 if t == 0:
-                    load[p][side].wait()
-                source = xs if side else xb
+                    gate_up_load[p, which, side].wait()
                 value = jnp.dot(
-                    source[rows, :], weight[side, :, cols], preferred_element_type=F32
+                    xb[batch_rows(t), :],
+                    weight[side, :, start : start + sub],
+                    preferred_element_type=F32,
                 )
-                to = slice(which * sub, (which + 1) * sub)
-                if side:
-                    send1[i, :, to] = value.astype(BF)
-                else:
-                    keep[i % slots, :, to] = value
+                for part in range(2):
+                    to = slice(edges[2 * part + which], edges[2 * part + which + 1])
+                    at = slice(part * quarter, (part + 1) * quarter)
+                    if side:
+                        send1[:, to] = value[:, at].astype(BF)
+                    else:
+                        keep[:, to] = value[:, at]
             if side:
-                both = slice(0, 2 * sub)
-                state["core", i] = push(send1.at[i, :, both], recv1.at[i, :, both], CORE)
-        if p == 0:
+                state["core", i] = push(send1.at[:, spans[i]], recv1.at[:, spans[i]], CORE)
+        if i == 0 or ITEMS[i - 1][0] != t:
             send_squares(t)
 
     def fold_core(i):
-        both = slice(0, 2 * chunks[i % CHUNKS][1])
+        quarter, edges = parts(i)
+        a, b = slice(edges[0], edges[2]), slice(edges[2], edges[4])
+
+        def total(first, last, cols):
+            rows = slice(first * blk, last * blk)
+            return keep[rows, cols] + recv1[rows, cols].astype(F32)
+
         state["core", i].wait_recv()
-        s = i % slots
-        send2[i, :, both] = (
-            keep[s, two : 2 * two, both] + recv1[i, two : 2 * two, both].astype(F32)
-        ).astype(BF)
-        state["second", i] = push_to(send2.at[i, :, both], recv2.at[i, :, both], first_peer)
-        keep[s, 0:two, both] += recv1[i, 0:two, both].astype(F32)
+        send2[:, a] = total(2, 4, a).astype(BF)
+        state["a2", i] = push(send2.at[:, a], recv2.at[:, a], XNBR)
+        send2[0:blk, b] = total(1, 2, b).astype(BF)
+        send2[blk:two, b] = total(3, 4, b).astype(BF)
+        state["b2", i] = push(send2.at[:, b], recv2.at[:, b], ZNBR)
+        keep[0:two, a] = total(0, 2, a)
+        keep[0:blk, b] = total(0, 1, b)
+        keep[two : 3 * blk, b] = total(2, 3, b)
 
     def fold_second(i):
-        both = slice(0, 2 * chunks[i % CHUNKS][1])
-        state["second", i].wait_recv()
-        s = i % slots
-        send3[i, :, both] = (
-            keep[s, blk:two, both] + recv2[i, blk:two, both].astype(F32)
-        ).astype(BF)
-        state["third", i] = push_to(send3.at[i, :, both], recv3.at[i, :, both], second_peer)
-        keep[s, 0:blk, both] += recv2[i, 0:blk, both].astype(F32)
-
-    def share_block(i, k):
-        cols = slice(0, chunks[i % CHUNKS][1])
-        sub = chunks[i % CHUNKS][1]
-        j = sibling_order[k]
-        state["hc", i, k] = push(
-            hb.at[i, k * blk : (k + 1) * blk, cols],
-            hb.at[i, j * blk : (j + 1) * blk, sub : 2 * sub],
-            CORE,
-        )
+        quarter, edges = parts(i)
+        a, b = slice(edges[0], edges[2]), slice(edges[2], edges[4])
+        state["a2", i].wait_recv()
+        send3[:, a] = (keep[blk:two, a] + recv2[blk:two, a].astype(F32)).astype(BF)
+        state["a3", i] = push(send3.at[:, a], recv3.at[:, a], ZNBR)
+        keep[0:blk, a] += recv2[0:blk, a].astype(F32)
+        state["b2", i].wait_recv()
+        send3[:, b] = (keep[two : 3 * blk, b] + recv2[blk:two, b].astype(F32)).astype(BF)
+        state["b3", i] = push(send3.at[:, b], recv3.at[:, b], XNBR)
+        keep[0:blk, b] += recv2[0:blk, b].astype(F32)
+
+    def own_units(i):
+        quarter, edges = parts(i)
+        return slice(edges[0], edges[2]), slice(edges[2], edges[4])
 
     def activate(i):
-        t, p = divmod(i, CHUNKS)
-        sub = chunks[p][1]
-        if p == 0:
+        t, p = ITEMS[i]
+        quarter, edges = parts(i)
+        if i == 0 or ITEMS[i - 1][0] != t:
             make_scale(t)
-        s = i % slots
-        state["third", i].wait_recv()
         factor = scale[token_rows(t, 0), 0:1]
-        gate = (keep[s, 0:blk, 0:sub] + recv3[i, :, 0:sub].astype(F32)) * factor
-        up = (keep[s, 0:blk, sub : 2 * sub] + recv3[i, :, sub : 2 * sub].astype(F32)) * factor
-        hb[i, 0:blk, 0:sub] = (gate / (1.0 + jnp.exp(-gate)) * up).astype(BF)
-        own = hb.at[i, 0:blk, 0:sub]
-        state["h1", i] = push_to(own, hb.at[i, blk:two, 0:sub], second_peer)
-        state["h2", i] = push_to(own, hb.at[i, two : 3 * blk, 0:sub], first_peer)
-        share_block(i, 0)
+        for part, name in enumerate(("a3", "b3")):
+            gates = slice(edges[2 * part], edges[2 * part + 1])
+            ups = slice(edges[2 * part + 1], edges[2 * part + 2])
+            state[name, i].wait_recv()
+            gate = (keep[0:blk, gates] + recv3[:, gates].astype(F32)) * factor
+            up = (keep[0:blk, ups] + recv3[:, ups].astype(F32)) * factor
+            hidden = gate / (1.0 + jnp.exp(-gate)) * up
+            hb[0:blk, edges[part] : edges[part + 1]] = hidden.astype(BF)
+        own = own_units(i)[0]
+        state["hz", i] = push(hb.at[0:blk, own], hb.at[blk:two, own], ZNBR)
+        state["hx", i] = push(hb.at[0:blk, own], hb.at[two : 3 * blk, own], XNBR)
 
     def relay(i):
-        sub = chunks[i % CHUNKS][1]
-        state["h1", i].wait_recv()
-        state["h3", i] = push_to(
-            hb.at[i, blk:two, 0:sub], hb.at[i, 3 * blk : 4 * blk, 0:sub], first_peer
-        )
-        share_block(i, 1)
-        state["h2", i].wait_recv()
-        share_block(i, 2)
+        quarter, edges = parts(i)
+        own, other = own_units(i)
+        first, last = slice(edges[0], edges[1]), slice(edges[1], edges[2])
+        far = slice(3 * blk, 4 * blk)
+        state["hz", i].wait_recv()
+        state["fx", i] = push(hb.at[blk:two, first], hb.at[far, first], XNBR)
+        state["hx", i].wait_recv()
+        state["fz", i] = push(hb.at[two : 3 * blk, last], hb.at[far, last], ZNBR)
+        near = slice(0, 3 * blk)
+        state["near", i] = push(hb.at[near, own], hb.at[near, other], CORE)
 
     def share_last(i):
-        state["h3", i].wait_recv()
-        share_block(i, 3)
+        own, other = own_units(i)
+        far = slice(3 * blk, 4 * blk)
+        state["fx", i].wait_recv()
+        state["fz", i].wait_recv()
+        state["far", i] = push(hb.at[far, own], hb.at[far, other], CORE)
 
     def down(i):
-        t, p = divmod(i, CHUNKS)
+        t, p = ITEMS[i]
         start, sub = chunks[p]
-        for k in range(4):
-            state["hc", i, k].wait_recv()
+        opens = i == 0 or ITEMS[i - 1][0] != t
+        state["near", i].wait_recv()
+        state["far", i].wait_recv()
         if t == 0:
             for load in down_load[p]:
                 load.wait()
         rows = slice(2 * start, 2 * start + 2 * sub)
-        batch = slice(t * half, (t + 1) * half)
         for part in (1, 0):
             cols = slice(part * out_w, (part + 1) * out_w)
-            value = jnp.dot(
-                hb[i, :, 0 : 2 * sub], wdb[rows, cols], preferred_element_type=F32
-            )
-            if p > 0:
-                value = acc[batch, cols] + value
-            if p == CHUNKS - 1 and part == 1:
-                dsend[batch, :] = value.astype(BF)
-                state["down", t] = push(dsend.at[batch], drecv.at[batch], OTHER)
+            value = jnp.dot(hb[:, spans[i]], wdb[rows, cols], preferred_element_type=F32)
+            if not opens:
+                value = acc[batch_rows(t), cols] + value
+            if part == 1 and not opens:
+                dsend[batch_rows(t), :] = value.astype(BF)
+                for k in range(4):
+                    at = t * half + k * blk
+                    state["down", t, k] = push(
+                        dsend.at[at : at + blk], other_out.at[token_rows(t, k)], OTHER
+                    )
             else:
-                acc[batch, cols] = value
-
-    steps = (multiply, fold_core, fold_second, activate, relay, share_last, down)
-    items = BATCHES * CHUNKS
-    for tick in range(items + len(steps) - 1):
-        for behind, step in enumerate(steps):
-            if 0 <= tick - behind < items:
-                step(tick - behind)
+                acc[batch_rows(t), cols] = value
+
+    steps = dict(
+        m=multiply, f=fold_core, s=fold_second, a=activate, r=relay, l=share_last, d=down
+    )
+    order = "m0f0m1f1s0m2f2a0s1m3f3r0a1s2l0r1a2d0l1s3r2d1a3l2r3d2l3d3"
+    for step, item in zip(order[0::2], order[1::2]):
+        steps[step](int(item))
 
     own_cols = pl.ds(pl.multiple_of(gr * out_w, out_w), out_w)
     for t in range(BATCHES):
-        state["down", t].wait_recv()
         for k in range(4):
             rows = slice(t * half + k * blk, t * half + (k + 1) * blk)
-            value = stream[rows, own_cols] + acc[rows, 0:out_w] + drecv[rows, :].astype(F32)
-            out[token_rows(t, k), :] = value.astype(BF)
+            at = token_rows(t, k)
+            own_out[at, :] = pbuf[at, own_cols] + acc[rows, 0:out_w]
+    for t in range(BATCHES):
+        for k in range(4):
+            state["down", t, k].wait_recv()
     for copy in sent:
         copy.wait_send()
 
@@ -457,32 +482,33 @@
     ff = gate_weight.shape[2]
     half = toks // BATCHES
     blk = half // 4
-    items = BATCHES * CHUNKS
-    most = 2 * max(sub for start, sub in chunks_of(ff // 2))
+    wide = columns_of(ff // 2)[-1].stop
     vm = pltpu.VMEM
     scratch = [
         vm((2, width, ff // 2), BF), vm((2, width, ff // 2), BF), vm((ff, width), BF),
         vm((8, toks, feat), BF), vm((toks // 2, width), BF), vm((8, 128), F32),
         vm((toks, width), F32), vm((toks, width), BF), vm((toks, width), BF),
-        vm((toks, width), F32), vm((toks, width), BF), vm((toks, width), BF),
-        vm((toks, width), F32),
+        vm((toks, width), BF), vm((toks, width), F32),
         vm((BATCHES, 8, toks), F32), vm((BATCHES, 7, 8, toks), F32), vm((toks, toks), F32),
-        vm((4, half, most), F32),
-        vm((items, half, most), BF), vm((items, half, most), BF),
-        vm((items, 2 * blk, most), BF), vm((items, 2 * blk, most), BF),
-        vm((items, blk, most), BF), vm((items, blk, most), BF),
-        vm((items, half, most), BF),
-        vm((toks, width // 2), BF), vm((toks, width // 2), BF),
-        pltpu.SemaphoreType.DMA((64,)),
-        pltpu.SemaphoreType.DMA((128,)), pltpu.SemaphoreType.DMA((128,)),
+        vm((half, wide), F32), vm((half, wide), BF), vm((half, wide), BF),
+        vm((2 * blk, wide), BF), vm((2 * blk, wide), BF),
+        vm((blk, wide), BF), vm((blk, wide), BF),
+        vm((half, wide), BF), vm((toks, width // 2), BF),
+        pltpu.SemaphoreType.DMA((48,)),
+        pltpu.SemaphoreType.DMA((96,)), pltpu.SemaphoreType.DMA((96,)),
     ]
     flops = 2 * toks * width * (8 * feat + 3 * ff)
     traffic = 2 * width * (8 * feat + 3 * ff)
-    result = pl.pallas_call(
+    own, other = pl.pallas_call(
         grid_kernel,
-        out_shape=jax.ShapeDtypeStruct((toks, width // 2), BF),
+        out_shape=(
+            jax.ShapeDtypeStruct((toks, width // 2), F32),
+            jax.ShapeDtypeStruct((toks, width // 2), BF),
+        ),
         in_specs=[pl.BlockSpec(memory_space=pl.ANY)] * 7,
-        out_specs=pl.BlockSpec(memory_space=pltpu.VMEM),
+        out_specs=(
+            pl.BlockSpec(memory_space=pltpu.VMEM), pl.BlockSpec(memory_space=pl.ANY)
+        ),
         scratch_shapes=scratch,
         compiler_params=pltpu.CompilerParams(
             collective_id=0, has_side_effects=True, vmem_limit_bytes=62 * 2**20
@@ -492,7 +518,7 @@
         attn_out, residual_in, out_weight, norm_gain.reshape(-1, 128),
         gate_weight, up_weight, down_weight,
     )
-    return result[:, None, :]
+    return (own + other.astype(F32)).astype(BF)[:, None, :]
 
 
 def solution(mesh):

time: 75.9 us -> 70.9 us (0.934); the launches traced: 75.8 us -> 69.5 us
  Pallas kernels: 74.2 us -> 67.8 us
  other arithmetic: 0 us -> 1.67 us
  local copies, waits for them, and re-layouts: 1.57 us -> 0 us
    pallas_call x1, Pallas kernels: 74.2 us -> 67.8 us  [fused(): pl.pallas_call(grid_kernel, out_shape=(jax.ShapeDtypeStruct((toks, width...]
    broadcast_in_dim x0 -> x1, other arithmetic: none -> 1.67 us  [fused(): return (own + other.astype(F32)).astype(BF)[:, None, :]]
    unnamed x1 -> x0, local copies, waits for them, and re-layouts: 1.57 us -> none
where the time goes in v4:
time: 70.9 us; the launch traced here: 69.5 us
  Pallas kernels  67.8 us (96%)
  other arithmetic  1.67 us (2%)
    pallas_call x1, Pallas kernels, fused(): pl.pallas_call(grid_kernel, out_shape=(jax.ShapeDtypeStruct((toks, width...  67.8 us
    broadcast_in_dim x1, other arithmetic, fused(): return (own + other.astype(F32)).astype(BF)[:, None, :]  1.67 us

profile of v4, /device:TPU:0, one launch (start us, length us, event | category | flops | bytes accessed | tf_op | source)
XLA Modules:
  0.0 69.5 jit_solution(9204260598439506366)
XLA Ops:
  0.0 67.8 %shard_map.73 = (f32[128,512]{1,0:T(8,128)}, bf16[128,512]{1,0:T(8,128)(2,1)}) custom-call(bf16[128,512]{1,0:T(8,128)(2,1)} %attn.1, bf16[1,64,1024]{2,1,0:T(8,128)(2,1)} %resid.1, bf16[1,4096,1024]{2,1,0:T(8,128)(2,1)} %wo.1, f32[64,128]{1,0:T(8,128)} %bitcast.3, bf16[1,1024,7168]{2,1,0:T(8,128)(2,1)} %wg.1, bf16[1,1024,7168]{2,1,0:T(8,128)(2,1)} %wu.1, ...), custom_call_target="tpu_custom_call" | custom-call | flops 6710886400 | bytes 52428800 | tf_op jit(solution)/shard_map/pallas_call | solution.py:502
  67.8 1.7 %fusion = bf16[128,1,512]{2,0,1:T(8,128)(2,1)} fusion(f32[128,512]{1,0:T(8,128)} %get-tuple-element.7, bf16[128,512]{1,0:T(8,128)(2,1)} %get-tuple-element.8), kind=kLoop, calls=%fused_computation.1 | loop fusion | flops 196608 | bytes 524288 | tf_op jit(solution)/shard_map/broadcast_in_dim | solution.py:521

commit v5 on v4

--- a/solution.py
+++ b/solution.py
@@ -126,8 +126,13 @@
 F32 = jnp.float32
 CORE, XNBR, ZNBR, OTHER = 1, 2, 4, 8
 BATCHES = 2
-SHARES = (3, 4)
-ITEMS = ((0, 0), (0, 1), (1, 1), (1, 0))
+SHARES = (1, 2, 2, 2)
+ITEMS = ((0, 0), (0, 1), (0, 2), (0, 3), (1, 3), (1, 2), (1, 1), (1, 0))
+ORDER = (
+    "g0m0g1f0m1g2f1s0m2g3f2m3s1a0f3g4s2m4a1r0f4s3g5a2r1l0",
+    "m5g6f5s4a3r2d0l1m6f6d1s5a4r3g7l2m7s6f7d2a5r4l3a6s7d3",
+    "r5l4r6a7d4l5l6r7d5l7d6d7",
+)
 
 
 def chunks_of(units):
@@ -239,7 +244,6 @@
             panel[d], wdb[d * feat : (d + 1) * feat, :], preferred_element_type=F32
         )
 
-    load_gate_up(0)
     own_load.wait()
     wo_load[0].wait()
     pbuf[...] = project(0)
@@ -252,7 +256,7 @@
     core_z = push(panel.at[4], panel.at[5], CORE)
     for d in (1, 2, 4, 3, 5, 6, 7):
         wo_load[d].wait()
-    for p in range(1, len(chunks)):
+    for p in (0, 1):
         load_gate_up(p)
     pbuf[...] += project(2)
     pbuf[...] += project(4)
@@ -279,21 +283,8 @@
         if t > 0:
             sent.pop().wait_send()
         from_other.append(push(psend.at[rows], precv.at[rows], OTHER))
-    down_load = []
-    for start, sub in chunks:
-        both = []
-        for side, owner in ((0, core), (1, 1 - core)):
-            first = pl.multiple_of(owner * units + start, 256)
-            to = 2 * start + side * sub
-            for part, holder in ((0, gr), (1, 1 - gr)):
-                cols = pl.ds(pl.multiple_of(holder * out_w, out_w), out_w)
-                both.append(
-                    fetch(
-                        wd.at[0, pl.ds(first, sub), cols],
-                        wdb.at[to : to + sub, part * out_w : (part + 1) * out_w],
-                    )
-                )
-        down_load.append(both)
+    for p in (2, 3):
+        load_gate_up(p)
     gain_load.wait()
     gain_row = jnp.concatenate([gainb[j : j + 1, :] for j in range(8)], axis=1)
 
@@ -326,6 +317,24 @@
         scale[batch_rows(t), :] = lax.rsqrt(spread[0:half, :] / D + 1e-05)
 
     state = {}
+    down_load = []
+
+    def load_down():
+        for start, sub in chunks:
+            both = []
+            for side, owner in ((0, core), (1, 1 - core)):
+                first = pl.multiple_of(owner * units + start, 256)
+                to = 2 * start + side * sub
+                for part, holder in ((0, gr), (1, 1 - gr)):
+                    cols = pl.ds(pl.multiple_of(holder * out_w, out_w), out_w)
+                    both.append(
+                        fetch(
+                            wd.at[0, pl.ds(first, sub), cols],
+                            wdb.at[to : to + sub, part * out_w : (part + 1) * out_w],
+                        )
+                    )
+            down_load.append(both)
+
 
     def parts(i):
         span = spans[i]
@@ -333,32 +342,39 @@
         edges = [span.start + n * quarter for n in range(5)]
         return quarter, edges
 
-    def multiply(i):
+    def opens(i):
+        return i == 0 or ITEMS[i - 1][0] != ITEMS[i][0]
+
+    def product(i, side):
         t, p = ITEMS[i]
         start, sub = chunks[p]
         quarter, edges = parts(i)
-        if i == 0 or ITEMS[i - 1][0] != t:
-            receive(t)
-        for side in (1, 0):
-            for which, weight in enumerate((wgb, wub)):
-                if t == 0:
-                    gate_up_load[p, which, side].wait()
-                value = jnp.dot(
-                    xb[batch_rows(t), :],
-                    weight[side, :, start : start + sub],
-                    preferred_element_type=F32,
-                )
-                for part in range(2):
-                    to = slice(edges[2 * part + which], edges[2 * part + which + 1])
-                    at = slice(part * quarter, (part + 1) * quarter)
-                    if side:
-                        send1[:, to] = value[:, at].astype(BF)
-                    else:
-                        keep[:, to] = value[:, at]
-            if side:
-                state["core", i] = push(send1.at[:, spans[i]], recv1.at[:, spans[i]], CORE)
-        if i == 0 or ITEMS[i - 1][0] != t:
-            send_squares(t)
+        for which, weight in enumerate((wgb, wub)):
+            if t == 0:
+                gate_up_load[p, which, side].wait()
+            value = jnp.dot(
+                xb[batch_rows(t), :],
+                weight[side, :, start : start + sub],
+                preferred_element_type=F32,
+            )
+            for part in range(2):
+                to = slice(edges[2 * part + which], edges[2 * part + which + 1])
+                at = slice(part * quarter, (part + 1) * quarter)
+                if side:
+                    send1[:, to] = value[:, at].astype(BF)
+                else:
+                    keep[:, to] = value[:, at]
+
+    def give(i):
+        if opens(i):
+            receive(ITEMS[i][0])
+        product(i, 1)
+        state["core", i] = push(send1.at[:, spans[i]], recv1.at[:, spans[i]], CORE)
+
+    def multiply(i):
+        product(i, 0)
+        if opens(i):
+            send_squares(ITEMS[i][0])
 
     def fold_core(i):
         quarter, edges = parts(i)
@@ -397,7 +413,7 @@
     def activate(i):
         t, p = ITEMS[i]
         quarter, edges = parts(i)
-        if i == 0 or ITEMS[i - 1][0] != t:
+        if opens(i):
             make_scale(t)
         factor = scale[token_rows(t, 0), 0:1]
         for part, name in enumerate(("a3", "b3")):
@@ -434,7 +450,7 @@
     def down(i):
         t, p = ITEMS[i]
         start, sub = chunks[p]
-        opens = i == 0 or ITEMS[i - 1][0] != t
+        closes = i + 1 == len(ITEMS) or opens(i + 1)
         state["near", i].wait_recv()
         state["far", i].wait_recv()
         if t == 0:
@@ -444,9 +460,9 @@
         for part in (1, 0):
             cols = slice(part * out_w, (part + 1) * out_w)
             value = jnp.dot(hb[:, spans[i]], wdb[rows, cols], preferred_element_type=F32)
-            if not opens:
+            if not opens(i):
                 value = acc[batch_rows(t), cols] + value
-            if part == 1 and not opens:
+            if part == 1 and closes:
                 dsend[batch_rows(t), :] = value.astype(BF)
                 for k in range(4):
                     at = t * half + k * blk
@@ -457,11 +473,14 @@
                 acc[batch_rows(t), cols] = value
 
     steps = dict(
-        m=multiply, f=fold_core, s=fold_second, a=activate, r=relay, l=share_last, d=down
-    )
-    order = "m0f0m1f1s0m2f2a0s1m3f3r0a1s2l0r1a2d0l1s3r2d1a3l2r3d2l3d3"
-    for step, item in zip(order[0::2], order[1::2]):
-        steps[step](int(item))
+        g=give, m=multiply, f=fold_core, s=fold_second,
+        a=activate, r=relay, l=share_last, d=down,
+    )
+    for line in ORDER:
+        for step, item in zip(line[0::2], line[1::2]):
+            steps[step](int(item))
+            if step + item == "m1":
+                load_down()
 
     own_cols = pl.ds(pl.multiple_of(gr * out_w, out_w), out_w)
     for t in range(BATCHES):
@@ -495,7 +514,7 @@
         vm((blk, wide), BF), vm((blk, wide), BF),
         vm((half, wide), BF), vm((toks, width // 2), BF),
         pltpu.SemaphoreType.DMA((48,)),
-        pltpu.SemaphoreType.DMA((96,)), pltpu.SemaphoreType.DMA((96,)),
+        pltpu.SemaphoreType.DMA((128,)), pltpu.SemaphoreType.DMA((128,)),
     ]
     flops = 2 * toks * width * (8 * feat + 3 * ff)
     traffic = 2 * width * (8 * feat + 3 * ff)

time: 70.9 us -> 72.2 us (1.018); the launches traced: 69.5 us -> 72.1 us
  Pallas kernels: 67.8 us -> 70.4 us
    pallas_call x1, Pallas kernels: 67.8 us -> 70.4 us  [fused(): pl.pallas_call(grid_kernel, out_shape=(jax.ShapeDtypeStruct((toks, width...]
where the time goes in v5:
time: 72.2 us; the launch traced here: 72.1 us
  Pallas kernels  70.4 us (98%)
  other arithmetic  1.67 us (2%)
    pallas_call x1, Pallas kernels, fused(): pl.pallas_call(grid_kernel, out_shape=(jax.ShapeDtypeStruct((toks, width...  70.4 us
    broadcast_in_dim x1, other arithmetic, fused(): return (own + other.astype(F32)).astype(BF)[:, None, :]  1.67 us

profile of v5, /device:TPU:0, one launch (start us, length us, event | category | flops | bytes accessed | tf_op | source)
XLA Modules:
  0.0 72.1 jit_solution(6454201345857589707)
XLA Ops:
  0.0 70.4 %shard_map.73 = (f32[128,512]{1,0:T(8,128)}, bf16[128,512]{1,0:T(8,128)(2,1)}) custom-call(bf16[128,512]{1,0:T(8,128)(2,1)} %attn.1, bf16[1,64,1024]{2,1,0:T(8,128)(2,1)} %resid.1, bf16[1,4096,1024]{2,1,0:T(8,128)(2,1)} %wo.1, f32[64,128]{1,0:T(8,128)} %bitcast.3, bf16[1,1024,7168]{2,1,0:T(8,128)(2,1)} %wg.1, bf16[1,1024,7168]{2,1,0:T(8,128)(2,1)} %wu.1, ...), custom_call_target="tpu_custom_call" | custom-call | flops 6710886400 | bytes 52428800 | tf_op jit(solution)/shard_map/pallas_call | solution.py:521
  70.4 1.7 %fusion = bf16[128,1,512]{2,0,1:T(8,128)(2,1)} fusion(f32[128,512]{1,0:T(8,128)} %get-tuple-element.7, bf16[128,512]{1,0:T(8,128)(2,1)} %get-tuple-element.8), kind=kLoop, calls=%fused_computation.1 | loop fusion | flops 196608 | bytes 524288 | tf_op jit(solution)/shard_map/broadcast_in_dim | solution.py:540
